TPU v7x, 1024 devices: a whole 4x4x32 slice. The times are simulated.
1024 devices in a mesh: wide: 16 (over x, z_hi, core), narrow: 64 (over y, z_lo).
Axes of the slice: x: 4, y: 4, z: 32 (z_hi: 2, z_lo: 16; z = z_hi * 16 + z_lo), core: 2. Of those that a mesh axis runs over, the one named last changes fastest.
Arguments:
- inputs: bfloat16 [131072, 4096], P(('wide', 'narrow')), may hold values from -6 to 6
- weight_codes: bfloat16 [4096, 512], P('wide'), may hold values from -127 to 127
- code_scales: float32 [4096, 2], P('wide'), may hold values from 0.00010625 to 0.000425
- key_cotangent: bfloat16 [131072, 512], P(('wide', 'narrow')), may hold values from -6 to 6
Outputs:
- keys: bfloat16 [131072, 512], P(('wide', 'narrow'))
- input_grad: bfloat16 [131072, 4096], P(('wide', 'narrow'))
- weight_grad: float32 [4096, 512], P(('wide', 'narrow'))
All inputs are finite; a program needn't handle non-finite values.
Results may differ from a plain program's by a relative error of at most 0.015.
Values may be sent and summed in bfloat16 or wider, within the bound.
No kernel may reach another device: no remote copies, remote signals or barrier semaphores. Data moves between devices by JAX's collectives and lax.ppermute only.
A program may use at most 64 MiB of HBM per device.

v0:
```python
import jax
import jax.numpy as jnp
from jax import lax
from jax.sharding import PartitionSpec as P


def dequantize(codes, scales):
    rows = codes.shape[0]
    blocks = codes.astype(jnp.float32).reshape(rows, scales.shape[1], -1) * scales[:, :, None]
    return blocks.reshape(rows, codes.shape[1]).astype(jnp.bfloat16)


def shards(inputs, weight_codes, code_scales, key_cotangent):
    pieces = (
        lax.all_gather(weight_codes, "wide", axis=0, tiled=True),
        lax.all_gather(code_scales.astype(jnp.bfloat16), "wide", axis=0, tiled=True).astype(
            jnp.float32
        ),
    )
    weight = dequantize(pieces[0], pieces[1])
    columns = inputs
    key_sums = jnp.dot(columns, weight, preferred_element_type=jnp.float32)
    weight = dequantize(pieces[0], pieces[1])
    block = lax.dot_general(
        key_cotangent, weight, (((1,), (1,)), ((), ())), preferred_element_type=jnp.float32
    )
    input_grad = block.astype(jnp.bfloat16)
    keys = key_sums.astype(jnp.bfloat16)
    columns = inputs
    term = jnp.dot(columns.T, key_cotangent, preferred_element_type=jnp.float32)
    group_sums = lax.psum_scatter(
        term.astype(jnp.bfloat16).astype(jnp.float32).astype(jnp.bfloat16),
        "wide",
        scatter_dimension=0,
        tiled=True,
    ).astype(jnp.float32)
    weight_grad = lax.psum_scatter(group_sums, "narrow", scatter_dimension=0, tiled=True)
    return (keys, input_grad, weight_grad)


def solution(mesh):
    return jax.shard_map(
        shards,
        mesh=mesh,
        in_specs=(
            P(("wide", "narrow"), None),
            P("wide", None),
            P("wide", None),
            P(("wide", "narrow"), None),
        ),
        out_specs=(
            P(("wide", "narrow"), None),
            P(("wide", "narrow"), None),
            P(("wide", "narrow"), None),
        ),
        check_vma=False,
    )
```

profile of v0, /device:TPU:516, one launch (start us, length us, event | category | flops | bytes accessed | tf_op | source)
XLA Modules:
  0.0 1115.9 jit_solution(1922533475329410942)
XLA Ops:
  7.2 0.0 copy-start
  7.2 0.0 reduce-scatter.2.cloned.1.call-start
  7.2 1.2 copy-done
  8.4 4.1 convolution_convert_fusion
  12.5 0.0 copy-start.2
  12.5 0.0 reduce-scatter.2.cloned.1.call-update
  12.5 0.0 all-gather.2.cloned.1.call-start
  12.6 0.7 all-gather.2.cloned.1.call-update
  13.3 0.0 copy-done.2
  13.3 54.9 %all_gather.7 = bf16[4096,2]{0,1:T(2,128)(2,1)S(1)} all-gather(bf16[256,2]{0,1:T(2,128)(2,1)S(1)} %convert_element_type.35), channel_id=1, replica_groups=mesh['wide'=16,'narrow'=64] {'wide'}, dimensions={0}, use_global_device_ids=true | all-gather | bytes 17408 | tf_op jit(solution)/shard_map/all_gather | solution.py:16
  68.2 0.4 copy.10
  68.6 4.9 mul.7
  73.5 0.0 copy-start.1
  73.5 4.2 copy.13
  77.8 1.3 dynamic-slice
  79.7 158.5 %reduce-scatter.2.cloned.1.call-done = bf16[256,512]{1,0:T(8,128)(2,1)} async-done(((bf16[4096,512]{1,0:T(8,128)(2,1)}), bf16[256,512]{1,0:T(8,128)(2,1)}) %reduce-scatter.2.cloned.1.call-update) | async-done | bytes 262160 | tf_op jit(solution)/shard_map/reduce_scatter | solution.py:31
  238.2 856.0 %all-reduce.2 = f32[256,512]{1,0:T(8,128)S(1)} all-reduce(bf16[256,512]{1,0:T(8,128)(2,1)} %reduce-scatter.2.cloned.1.call-done), channel_id=3, replica_groups=mesh['wide'=16,'narrow'=64] {'narrow'}, use_global_device_ids=true, to_apply=%region_1.0.clone | all-reduce | flops 131072 | bytes 786432
  1094.2 0.6 constant_dynamic-slice_fusion
  1094.8 0.0 all-gather.2.cloned.1.call-done
  1094.8 0.0 copy-done.1
  1094.9 5.8 fusion
  1100.7 1.3 copy.12
  1102.0 6.3 fusion.1
  1108.3 0.8 copy.11
  (1 shorter events, 0.0 us)
Async XLA Ops:
  7.2 1.2 copy-start
  7.2 231.0 %reduce-scatter.2.cloned.1.call-start = ((), (), s32[]{:S(2)}) async-start(), calls=%async_computation.2 | async-start | bytes 4456448 | tf_op jit(solution)/shard_map/reduce_scatter | solution.py:31
  12.5 0.8 copy-start.2
  12.5 1082.3 %all-gather.2.cloned.1.call-start = ((), (), s32[]{:S(2)}) async-start(), calls=%async_computation.1 | async-start | bytes 4456448 | tf_op jit(solution)/shard_map/all_gather | solution.py:15
  73.5 1021.3 %copy-start.1 = (bf16[128,512]{1,0:T(8,128)(2,1)S(1)}, bf16[128,512]{1,0:T(8,128)(2,1)}, u32[]{:S(2)}) copy-start(bf16[128,512]{1,0:T(8,128)(2,1)} %param.7) | copy-start | bytes 393220
Sparse Core Ops, SparseCore 0:
  14.1 224.0 reduce-scatter.1
  243.4 188.4 all-gather.1
where the time goes:
time: 1120 us
  blocking collectives  911 us (81%)
  waiting for transfers between devices  159 us (14%)
  matrix products  16.3 us (1%)
  between operations  14.8 us (1%)
  local copies, waits for them, and re-layouts  14.7 us (1%)
    unnamed x1, blocking collectives  856 us
    reduce_scatter x1, waiting for transfers between devices, shards(): lax.psum_scatter(term.astype(jnp.bfloat16).astype(jnp.float32).astype(jnp...  159 us
    all_gather x1, blocking collectives, shards(): lax.all_gather(code_scales.astype(jnp.bfloat16), 'wide', axis=0, tiled=True)  54.9 us
  transfers between devices with their start and end apart: 2, of which 1 were waited for; matrix products, arithmetic and copies ran while one was open for 1% of the time, Pallas kernels for 0%

commit v1 on v0

v1 whole, which is shorter than its diff:
```python
import functools

import jax
import jax.numpy as jnp
from jax import lax
from jax.experimental import pallas as pl
from jax.experimental.pallas import tpu as pltpu
from jax.sharding import PartitionSpec as P

BOTH = ("wide", "narrow")
BF16, F32 = jnp.bfloat16, jnp.float32
VMEM_LIMIT = 48 * 1024 * 1024


def flat(x, y, z, c):
    x, y, z = x % 4, y % 4, z % 32
    return ((x * 2 + z // 16) * 2 + c) * 64 + y * 16 + z % 16


def pairs(move):
    return [
        (flat(x, y, z, c), flat(*move(x, y, z, c)))
        for x in range(4)
        for y in range(4)
        for z in range(32)
        for c in range(2)
    ]


def first_axis(d):
    return pairs(lambda x, y, z, c: (x + d, y, z, c) if c == 0 else (x, y + d, z, c))


def second_axis(d):
    return pairs(lambda x, y, z, c: (x, y + d, z, c) if c == 0 else (x + d, y, z, c))


def core_swap():
    return pairs(lambda x, y, z, c: (x, y, z, 1 - c))


def half_swap():
    return pairs(lambda x, y, z, c: (x, y, z + 8 if z % 16 >= 8 else z - 8, c))


def z_groups():
    return [
        [flat(x, y, z, c) for z in range(32)] for x in range(4) for y in range(4) for c in range(2)
    ]


def coords():
    w, n = lax.axis_index("wide"), lax.axis_index("narrow")
    return lax.div(w, 4), lax.div(n, 16), lax.rem(lax.div(w, 2), 2), lax.rem(w, 2)


def up(v, d):
    return lax.rem(v + d, 4)


def down(v, d):
    return lax.rem(v + 4 - d, 4)


def rows_at(i, size):
    return pl.ds(pl.multiple_of(i * size, size), size)


def call(body, outs, ins, scratch=(), flops=0):
    moved = sum(a.size * a.dtype.itemsize for a in (*ins, *outs))
    return pl.pallas_call(
        body,
        out_shape=outs,
        in_specs=[pl.BlockSpec(memory_space=pltpu.VMEM)] * len(ins),
        out_specs=[pl.BlockSpec(memory_space=pltpu.VMEM)] * len(outs),
        scratch_shapes=scratch,
        compiler_params=pltpu.CompilerParams(vmem_limit_bytes=VMEM_LIMIT),
        cost_estimate=pl.CostEstimate(flops=flops, bytes_accessed=moved, transcendentals=0),
    )(*ins)


def term_body(other, x_ref, k_ref, out_ref):
    _, _, _, c = coords()
    cc = 1 - c if other else c
    for b in range(8):
        block = x_ref[:, rows_at(2 * b + cc, 256)]
        out_ref[b * 256 : (b + 1) * 256, :] = lax.dot_general(
            block, k_ref[...], (((0,), (0,)), ((), ())), preferred_element_type=F32
        ).astype(out_ref.dtype)


def split_first_body(keep_ref, got_ref, mine_ref, *out_refs):
    x, y, _, c = coords()
    for d in range(4):
        ref = mine_ref if d == 0 else out_refs[d - 1]
        for j in range(4):
            to_x = jnp.where(c == 0, up(x, d), j)
            to_y = jnp.where(c == 0, j, up(y, d))
            for h in range(2):
                rows = rows_at((to_x * 2 + h) * 4 + to_y, 64)
                total = keep_ref[rows, :].astype(F32) + got_ref[rows, :].astype(F32)
                ref[j, h] = total.astype(ref.dtype)


def split_second_body(own_ref, a_ref, b_ref, c_ref, mine_ref, *out_refs):
    x, y, _, c = coords()
    me = jnp.where(c == 0, y, x)
    for e in range(4):
        ref = mine_ref if e == 0 else out_refs[e - 1]
        j = up(me, e)
        total = own_ref[j] + a_ref[j].astype(F32) + b_ref[j].astype(F32) + c_ref[j].astype(F32)
        ref[...] = total.astype(ref.dtype)


def project_body(x_ref, k_ref, *refs):
    pieces, (keys_ref, grad_ref, weight_ref) = refs[:8], refs[8:]
    x, y, zh, c = coords()
    for s in range(2):
        core = c if s == 0 else 1 - c
        for e in range(4):
            for d in range(4):
                at_x = jnp.where(core == 0, down(x, d), down(x, e))
                at_y = jnp.where(core == 0, down(y, e), down(y, d))
                for r in range(2):
                    h = zh if r == 0 else 1 - zh
                    rows = rows_at(((at_x * 2 + h) * 2 + core) * 4 + at_y, 64)
                    weight_ref[rows, :] = pieces[s * 4 + e][d, r]
    keys_ref[...] = jnp.dot(x_ref[...], weight_ref[...], preferred_element_type=F32).astype(BF16)
    for b in range(8):
        rows = slice(b * 512, (b + 1) * 512)
        grad_ref[:, rows] = lax.dot_general(
            k_ref[...], weight_ref[rows, :], (((1,), (1,)), ((), ())), preferred_element_type=F32
        ).astype(BF16)


def dequantize(codes, scales):
    rows = codes.shape[0]
    blocks = codes.astype(F32).reshape(rows, scales.shape[1], -1) * scales[:, :, None]
    return blocks.reshape(rows, codes.shape[1]).astype(BF16)


def shape(dims, dtype):
    return jax.ShapeDtypeStruct(dims, dtype)


def shards(inputs, weight_codes, code_scales, key_cotangent):
    y = coords()[1]
    swap = core_swap()

    weight = dequantize(weight_codes, code_scales)
    quarter = lax.dynamic_slice(weight, (y * 64, 0), (64, 512))
    other = lax.ppermute(quarter, BOTH, half_swap())

    flops = 2 * 128 * 2048 * 512
    sent = call(
        functools.partial(term_body, True),
        [shape((2048, 512), BF16)],
        (inputs, key_cotangent),
        flops=flops,
    )[0]
    got = lax.ppermute(sent, BOTH, swap)
    keep = call(
        functools.partial(term_body, False),
        [shape((2048, 512), F32)],
        (inputs, key_cotangent),
        flops=flops,
    )[0]

    base = jnp.stack([quarter, other])
    line = jnp.stack([base] + [lax.ppermute(base, BOTH, first_axis(d)) for d in (1, 2, 3)])

    chunk = (4, 2, 64, 512)
    mine, *outs = call(
        split_first_body, [shape(chunk, F32)] + [shape(chunk, BF16)] * 3, (keep, got)
    )
    ins = [lax.ppermute(o, BOTH, first_axis(d)) for d, o in zip((1, 2, 3), outs)]

    plane = [line] + [lax.ppermute(line, BOTH, second_axis(d)) for d in (1, 2, 3)]

    chunk = (2, 64, 512)
    mine, *outs = call(
        split_second_body, [shape(chunk, F32)] + [shape(chunk, BF16)] * 3, (mine, *ins)
    )
    ins = [lax.ppermute(o, BOTH, second_axis(d)) for d, o in zip((1, 2, 3), outs)]
    swapped = [lax.ppermute(p, BOTH, swap) for p in plane]

    column = mine + sum(i.astype(F32) for i in ins)
    column = column.astype(BF16).reshape(32, 4, 4, 128).reshape(32, 16, 128)
    column = lax.all_to_all(column, BOTH, 0, 0, tiled=True, axis_index_groups=z_groups())
    weight_grad = jnp.sum(column.astype(F32), axis=0).reshape(4, 512)

    keys, input_grad = call(
        project_body,
        [shape((128, 512), BF16), shape((128, 4096), BF16)],
        (inputs, key_cotangent, *plane, *swapped),
        scratch=[pltpu.VMEM((4096, 512), BF16)],
        flops=4 * 128 * 4096 * 512,
    )
    return keys, input_grad, weight_grad


def solution(mesh):
    return jax.shard_map(
        shards,
        mesh=mesh,
        in_specs=(P(BOTH, None), P("wide", None), P("wide", None), P(BOTH, None)),
        out_specs=(P(BOTH, None), P(BOTH, None), P(BOTH, None)),
        check_vma=False,
    )
```

time: 1120 us -> 138 us (0.12)
  the two profiles are of different devices: /device:TPU:516 before, /device:TPU:24 now
where the time goes in v1:
time: 138 us; the launch traced here: 136 us
  starting transfers between devices  91.8 us (67%)
  waiting for transfers between devices  24.6 us (18%)
  local copies, waits for them, and re-layouts  8.56 us (6%)
  Pallas kernels  8.52 us (6%)
    ppermute x1, starting transfers between devices, shards(): other = lax.ppermute(quarter, BOTH, half_swap())  23 us
    all_to_all x1, starting transfers between devices, shards(): lax.all_to_all(column, BOTH, 0, 0, tiled=True, axis_index_groups=z_groups())  14.5 us
    all_to_all x1, waiting for transfers between devices, shards(): lax.all_to_all(column, BOTH, 0, 0, tiled=True, axis_index_groups=z_groups())  13.5 us
    ppermute x3, starting transfers between devices, shards(): lax.ppermute(base, BOTH, first_axis(d))  12 us
    ppermute x3, starting transfers between devices, shards(): lax.ppermute(o, BOTH, first_axis(d))  11.4 us
    ppermute x3, starting transfers between devices, shards(): lax.ppermute(line, BOTH, second_axis(d))  10.5 us
    ppermute x3, starting transfers between devices, shards(): lax.ppermute(o, BOTH, second_axis(d))  9.92 us
    ppermute x4, starting transfers between devices, shards(): swapped = [lax.ppermute(p, BOTH, swap) for p in plane]  8.65 us
  transfers between devices with their start and end apart: 19, of which 4 were waited for; matrix products, arithmetic and copies ran while one was open for 2% of the time, Pallas kernels for 3%

profile of v1, /device:TPU:24, one launch (start us, length us, event | category | flops | bytes accessed | tf_op | source)
XLA Modules:
  0.0 135.6 jit_solution(14143058011212160613)
XLA Ops:
  0.6 0.0 copy-start.1
  0.6 1.2 copy-done.1
  1.9 0.9 copy-done.3
  2.8 0.7 shard_map.69
  3.5 1.9 %collective-permute-start.11 = (bf16[2048,512]{1,0:T(8,128)(2,1)S(1)}, bf16[2048,512]{1,0:T(8,128)(2,1)S(1)}, u32[]{:S(2)}, u32[]{:S(2)}) collective-permute-start(bf16[2048,512]{1,0:T(8,128)(2,1)S(1)} %shard_map.69), channel_id=1, source_target_pairs={{0,64},{64,0},{1,65},{65,1},{2,66},{66,2},{3,67},{67,3},{4,68},{68... | collective-permute-start | bytes 6291464 | tf_op jit(solution)/shard_map/ppermute | solution.py:161
  5.4 0.7 shard_map.68.keep_ref
  6.2 2.0 %copy-done = f32[2048,512]{1,0:T(8,128)} copy-done((f32[2048,512]{1,0:T(8,128)}, f32[2048,512]{1,0:T(8,128)S(1)}, u32[]{:S(2)}) %copy-start) | copy-done | bytes 4194328
  8.1 1.4 %collective-permute-done.11.got_ref = bf16[2048,512]{1,0:T(8,128)(2,1)S(1)} collective-permute-done((bf16[2048,512]{1,0:T(8,128)(2,1)S(1)}, bf16[2048,512]{1,0:T(8,128)(2,1)S(1)}, u32[]{:S(2)}, u32[]{:S(2)}) %collective-permute-start.11) | collective-permute-done | bytes 2097184 | tf_op jit(solution)/shard_map/ppermute | solution.py:161
  9.6 3.5 %shard_map.70 = (f32[4,2,64,512]{3,2,1,0:T(8,128)S(1)}, bf16[4,2,64,512]{3,2,1,0:T(8,128)(2,1)}, bf16[4,2,64,512]{3,2,1,0:T(8,128)(2,1)}, bf16[4,2,64,512]{3,2,1,0:T(8,128)(2,1)S(1)}) custom-call(f32[2048,512]{1,0:T(8,128)} %copy-done, bf16[2048,512]{1,0:T(8,128)(2,1)S(1)} %collective-permute-done.11.got_ref), custom_call_target="tpu_custom_call" | custom-call | bytes 8912896 | tf_op jit(solution)/shard_map/pallas_call | solution.py:71
  13.0 3.4 %collective-permute-start.12 = (bf16[4,2,64,512]{3,2,1,0:T(8,128)(2,1)}, bf16[4,2,64,512]{3,2,1,0:T(8,128)(2,1)S(1)}, u32[]{:S(2)}, u32[]{:S(2)}) collective-permute-start(bf16[4,2,64,512]{3,2,1,0:T(8,128)(2,1)} %get-tuple-element.16), channel_id=1, source_target_pairs={{0,256},{64,80},{1,257},{65,81},{2,258},{66,82},{3,259},{67,83},{4... | collective-permute-start | bytes 1572872 | tf_op jit(solution)/shard_map/ppermute | solution.py:176
  16.4 4.6 %collective-permute-start.13 = (bf16[4,2,64,512]{3,2,1,0:T(8,128)(2,1)}, bf16[4,2,64,512]{3,2,1,0:T(8,128)(2,1)S(1)}, u32[]{:S(2)}, u32[]{:S(2)}) collective-permute-start(bf16[4,2,64,512]{3,2,1,0:T(8,128)(2,1)} %get-tuple-element.17), channel_id=1, source_target_pairs={{0,512},{64,96},{1,513},{65,97},{2,514},{66,98},{3,515},{67,99},{4... | collective-permute-start | bytes 1572872 | tf_op jit(solution)/shard_map/ppermute | solution.py:176
  21.1 3.3 %collective-permute-start.14 = (bf16[4,2,64,512]{3,2,1,0:T(8,128)(2,1)S(1)}, bf16[4,2,64,512]{3,2,1,0:T(8,128)(2,1)S(1)}, u32[]{:S(2)}, u32[]{:S(2)}) collective-permute-start(bf16[4,2,64,512]{3,2,1,0:T(8,128)(2,1)S(1)} %get-tuple-element.18), channel_id=1, source_target_pairs={{0,768},{64,112},{1,769},{65,113},{2,770},{66,114},{3,771},{67,115... | collective-permute-start | bytes 1572872 | tf_op jit(solution)/shard_map/ppermute | solution.py:176
  24.5 0.1 copy.7
  24.6 0.3 mul.14
  24.9 0.8 copy.8
  25.8 0.9 fusion
  26.7 23.0 %collective-permute-start = (bf16[64,512]{1,0:T(8,128)(2,1)S(1)}, bf16[64,512]{1,0:T(8,128)(2,1)S(1)}, u32[]{:S(2)}, u32[]{:S(2)}) collective-permute-start(bf16[64,512]{1,0:T(8,128)(2,1)S(1)} %fusion), channel_id=1, source_target_pairs={{0,136},{64,200},{1,137},{65,201},{2,138},{66,202},{3,139},{67,203... | collective-permute-start | bytes 196616 | tf_op jit(solution)/shard_map/ppermute | solution.py:152
  49.7 8.1 %collective-permute-done = bf16[64,512]{1,0:T(8,128)(2,1)S(1)} collective-permute-done((bf16[64,512]{1,0:T(8,128)(2,1)S(1)}, bf16[64,512]{1,0:T(8,128)(2,1)S(1)}, u32[]{:S(2)}, u32[]{:S(2)}) %collective-permute-start) | collective-permute-done | bytes 65568 | tf_op jit(solution)/shard_map/ppermute | solution.py:152
  57.8 4.9 %collective-permute-start.2 = (bf16[2,64,512]{2,1,0:T(8,128)(2,1)S(1)}, bf16[2,64,512]{2,1,0:T(8,128)(2,1)S(1)}, u32[]{:S(2)}, u32[]{:S(2)}) collective-permute-start(bf16[2,64,512]{2,1,0:T(8,128)(2,1)S(1)} %get-tuple-element.24), channel_id=1, source_target_pairs={{0,512},{64,96},{1,513},{65,97},{2,514},{66,98},{3,515},{67,99},{4... | collective-permute-start | bytes 393224 | tf_op jit(solution)/shard_map/ppermute | solution.py:170
  62.8 2.5 %collective-permute-start.1 = (bf16[2,64,512]{2,1,0:T(8,128)(2,1)S(1)}, bf16[2,64,512]{2,1,0:T(8,128)(2,1)S(1)}, u32[]{:S(2)}, u32[]{:S(2)}) collective-permute-start(bf16[2,64,512]{2,1,0:T(8,128)(2,1)S(1)} %get-tuple-element.24), channel_id=1, source_target_pairs={{0,256},{64,80},{1,257},{65,81},{2,258},{66,82},{3,259},{67,83},{4... | collective-permute-start | bytes 393224 | tf_op jit(solution)/shard_map/ppermute | solution.py:170
  65.3 4.6 %collective-permute-start.3 = (bf16[2,64,512]{2,1,0:T(8,128)(2,1)S(1)}, bf16[2,64,512]{2,1,0:T(8,128)(2,1)S(1)}, u32[]{:S(2)}, u32[]{:S(2)}) collective-permute-start(bf16[2,64,512]{2,1,0:T(8,128)(2,1)S(1)} %get-tuple-element.24), channel_id=1, source_target_pairs={{0,768},{64,112},{1,769},{65,113},{2,770},{66,114},{3,771},{67,115... | collective-permute-start | bytes 393224 | tf_op jit(solution)/shard_map/ppermute | solution.py:170
  69.9 0.0 copy-start.5
  69.9 0.8 copy-done.5
  70.7 1.0 copy-done.6
  71.7 0.2 shard_map.71
  71.9 2.9 %collective-permute-start.15 = (bf16[2,64,512]{2,1,0:T(8,128)(2,1)S(1)}, bf16[2,64,512]{2,1,0:T(8,128)(2,1)S(1)}, u32[]{:S(2)}, u32[]{:S(2)}) collective-permute-start(bf16[2,64,512]{2,1,0:T(8,128)(2,1)S(1)} %get-tuple-element.20), channel_id=1, source_target_pairs={{0,16},{64,320},{1,17},{65,321},{2,18},{66,322},{3,19},{67,323},{4... | collective-permute-start | bytes 393224 | tf_op jit(solution)/shard_map/ppermute | solution.py:184
  74.8 3.8 %collective-permute-start.16 = (bf16[2,64,512]{2,1,0:T(8,128)(2,1)S(1)}, bf16[2,64,512]{2,1,0:T(8,128)(2,1)S(1)}, u32[]{:S(2)}, u32[]{:S(2)}) collective-permute-start(bf16[2,64,512]{2,1,0:T(8,128)(2,1)S(1)} %get-tuple-element.21), channel_id=1, source_target_pairs={{0,32},{64,576},{1,33},{65,577},{2,34},{66,578},{3,35},{67,579},{4... | collective-permute-start | bytes 393224 | tf_op jit(solution)/shard_map/ppermute | solution.py:184
  78.6 0.0 collective-permute-done.2
  78.6 3.2 %collective-permute-start.17 = (bf16[2,64,512]{2,1,0:T(8,128)(2,1)S(1)}, bf16[2,64,512]{2,1,0:T(8,128)(2,1)S(1)}, u32[]{:S(2)}, u32[]{:S(2)}) collective-permute-start(bf16[2,64,512]{2,1,0:T(8,128)(2,1)S(1)} %get-tuple-element.22), channel_id=1, source_target_pairs={{0,48},{64,832},{1,49},{65,833},{2,50},{66,834},{3,51},{67,835},{4... | collective-permute-start | bytes 393224 | tf_op jit(solution)/shard_map/ppermute | solution.py:184
  81.9 0.0 collective-permute-done.1
  81.9 0.0 collective-permute-done.3
  81.9 0.1 pad_maximum_fusion.refs_0_
  82.0 2.2 %collective-permute-start.6 = (bf16[4,2,64,512]{3,2,1,0:T(8,128)(2,1)S(1)}, bf16[4,2,64,512]{3,2,1,0:T(8,128)(2,1)S(1)}, u32[]{:S(2)}, u32[]{:S(2)}) collective-permute-start(bf16[4,2,64,512]{3,2,1,0:T(8,128)(2,1)S(1)} %pad_maximum_fusion.refs_0_), channel_id=1, source_target_pairs={{0,48},{64,832},{1,49},{65,833},{2,50},{66,834},{3,51},{67,835},{4... | collective-permute-start | bytes 1572872 | tf_op jit(solution)/shard_map/ppermute | solution.py:178
  84.2 5.0 %collective-permute-start.5 = (bf16[4,2,64,512]{3,2,1,0:T(8,128)(2,1)S(1)}, bf16[4,2,64,512]{3,2,1,0:T(8,128)(2,1)S(1)}, u32[]{:S(2)}, u32[]{:S(2)}) collective-permute-start(bf16[4,2,64,512]{3,2,1,0:T(8,128)(2,1)S(1)} %pad_maximum_fusion.refs_0_), channel_id=1, source_target_pairs={{0,32},{64,576},{1,33},{65,577},{2,34},{66,578},{3,35},{67,579},{4... | collective-permute-start | bytes 1572872 | tf_op jit(solution)/shard_map/ppermute | solution.py:178
  89.2 0.0 collective-permute-done.15
  89.2 3.3 %collective-permute-start.4 = (bf16[4,2,64,512]{3,2,1,0:T(8,128)(2,1)S(1)}, bf16[4,2,64,512]{3,2,1,0:T(8,128)(2,1)S(1)}, u32[]{:S(2)}, u32[]{:S(2)}) collective-permute-start(bf16[4,2,64,512]{3,2,1,0:T(8,128)(2,1)S(1)} %pad_maximum_fusion.refs_0_), channel_id=1, source_target_pairs={{0,16},{64,320},{1,17},{65,321},{2,18},{66,322},{3,19},{67,323},{4... | collective-permute-start | bytes 1572872 | tf_op jit(solution)/shard_map/ppermute | solution.py:178
  92.5 0.0 collective-permute-done.16
  92.5 0.1 add_convert_fusion
  92.6 0.7 reshape_reshape.3
  93.3 14.5 %all-to-all-start = ((bf16[32,16,128]{2,1,0:T(8,128)(2,1)}), bf16[32,16,128]{2,1,0:T(8,128)(2,1)S(1)}, u32[]{:S(2)}, u32[]{:S(2)}) async-start(bf16[32,16,128]{2,1,0:T(8,128)(2,1)} %reshape_reshape.3), calls=%async_computation | async-start | bytes 262144 | tf_op jit(solution)/shard_map/all_to_all | solution.py:189
  107.8 1.9 %collective-permute-start.7 = (bf16[4,2,64,512]{3,2,1,0:T(8,128)(2,1)S(1)}, bf16[4,2,64,512]{3,2,1,0:T(8,128)(2,1)S(1)}, u32[]{:S(2)}, u32[]{:S(2)}) collective-permute-start(bf16[4,2,64,512]{3,2,1,0:T(8,128)(2,1)S(1)} %pad_maximum_fusion.refs_0_), channel_id=1, source_target_pairs={{0,64},{64,0},{1,65},{65,1},{2,66},{66,2},{3,67},{67,3},{4,68},{68... | collective-permute-start | bytes 1572872 | tf_op jit(solution)/shard_map/ppermute | solution.py:185
  109.7 2.4 %collective-permute-start.10 = (bf16[4,2,64,512]{3,2,1,0:T(8,128)(2,1)S(1)}, bf16[4,2,64,512]{3,2,1,0:T(8,128)(2,1)S(1)}, u32[]{:S(2)}, u32[]{:S(2)}) collective-permute-start(bf16[4,2,64,512]{3,2,1,0:T(8,128)(2,1)S(1)} %collective-permute-done.6.refs_3_), channel_id=1, source_target_pairs={{0,64},{64,0},{1,65},{65,1},{2,66},{66,2},{3,67},{67,3},{4,68},{68... | collective-permute-start | bytes 1572872 | tf_op jit(solution)/shard_map/ppermute | solution.py:185
  112.2 1.9 %collective-permute-start.9 = (bf16[4,2,64,512]{3,2,1,0:T(8,128)(2,1)S(1)}, bf16[4,2,64,512]{3,2,1,0:T(8,128)(2,1)S(1)}, u32[]{:S(2)}, u32[]{:S(2)}) collective-permute-start(bf16[4,2,64,512]{3,2,1,0:T(8,128)(2,1)S(1)} %collective-permute-done.5.refs_2_), channel_id=1, source_target_pairs={{0,64},{64,0},{1,65},{65,1},{2,66},{66,2},{3,67},{67,3},{4,68},{68... | collective-permute-start | bytes 1572872 | tf_op jit(solution)/shard_map/ppermute | solution.py:185
  114.1 2.4 %collective-permute-start.8 = (bf16[4,2,64,512]{3,2,1,0:T(8,128)(2,1)S(1)}, bf16[4,2,64,512]{3,2,1,0:T(8,128)(2,1)S(1)}, u32[]{:S(2)}, u32[]{:S(2)}) collective-permute-start(bf16[4,2,64,512]{3,2,1,0:T(8,128)(2,1)S(1)} %collective-permute-done.4.refs_1_), channel_id=1, source_target_pairs={{0,64},{64,0},{1,65},{65,1},{2,66},{66,2},{3,67},{67,3},{4,68},{68... | collective-permute-start | bytes 1572872 | tf_op jit(solution)/shard_map/ppermute | solution.py:185
  116.5 1.5 %collective-permute-done.8.refs_5_ = bf16[4,2,64,512]{3,2,1,0:T(8,128)(2,1)S(1)} collective-permute-done((bf16[4,2,64,512]{3,2,1,0:T(8,128)(2,1)S(1)}, bf16[4,2,64,512]{3,2,1,0:T(8,128)(2,1)S(1)}, u32[]{:S(2)}, u32[]{:S(2)}) %collective-permute-start.8) | collective-permute-done | bytes 524320 | tf_op jit(solution)/shard_map/ppermute | solution.py:185
  118.0 3.3 %shard_map.67 = (bf16[128,512]{1,0:T(8,128)(2,1)}, bf16[128,4096]{1,0:T(8,128)(2,1)}) custom-call(bf16[128,4096]{1,0:T(8,128)(2,1)S(1)} %copy-done.2, bf16[128,512]{1,0:T(8,128)(2,1)S(1)} %copy-done.4, bf16[4,2,64,512]{3,2,1,0:T(8,128)(2,1)S(1)} %pad_maximum_fusion.refs_0_, bf16[4,2,64,512]{3,2,1,0:T(8,128)(2,1)S(1)} %collective-permute-done.4.refs_1_, ...), custom_call_target="tpu_custom_call" | custom-call | flops 1073741824 | bytes 6553600 | tf_op jit(solution)/shard_map/pallas_call | solution.py:71
  121.4 13.5 %all-to-all-done = bf16[32,16,128]{2,1,0:T(8,128)(2,1)S(1)} async-done(((bf16[32,16,128]{2,1,0:T(8,128)(2,1)}), bf16[32,16,128]{2,1,0:T(8,128)(2,1)S(1)}, u32[]{:S(2)}, u32[]{:S(2)}) %all-to-all-start) | async-done | bytes 131104 | tf_op jit(solution)/shard_map/all_to_all | solution.py:189
  134.9 0.6 reshape.13
  (21 shorter events, 0.1 us)
Async XLA Ops:
  0.6 1.2 copy-start.1
  1.9 0.9 copy-start.3
  3.5 6.1 %collective-permute-start.11 = (bf16[2048,512]{1,0:T(8,128)(2,1)S(1)}, bf16[2048,512]{1,0:T(8,128)(2,1)S(1)}, u32[]{:S(2)}, u32[]{:S(2)}) collective-permute-start(bf16[2048,512]{1,0:T(8,128)(2,1)S(1)} %shard_map.69), channel_id=1, source_target_pairs={{0,64},{64,0},{1,65},{65,1},{2,66},{66,2},{3,67},{67,3},{4,68},{68... | collective-permute-start | bytes 6291464 | tf_op jit(solution)/shard_map/ppermute | solution.py:161
  6.2 2.0 %copy-start = (f32[2048,512]{1,0:T(8,128)}, f32[2048,512]{1,0:T(8,128)S(1)}, u32[]{:S(2)}) copy-start(f32[2048,512]{1,0:T(8,128)S(1)} %shard_map.68.keep_ref) | copy-start | bytes 12582916
  8.1 16.3 %copy-start.7 = (f32[256,2]{0,1:T(2,128)S(1)}, f32[256,2]{0,1:T(2,128)}, u32[]{:S(2)}) copy-start(f32[256,2]{0,1:T(2,128)} %param.6) | copy-start | bytes 6148
  13.0 52.2 %collective-permute-start.12 = (bf16[4,2,64,512]{3,2,1,0:T(8,128)(2,1)}, bf16[4,2,64,512]{3,2,1,0:T(8,128)(2,1)S(1)}, u32[]{:S(2)}, u32[]{:S(2)}) collective-permute-start(bf16[4,2,64,512]{3,2,1,0:T(8,128)(2,1)} %get-tuple-element.16), channel_id=1, source_target_pairs={{0,256},{64,80},{1,257},{65,81},{2,258},{66,82},{3,259},{67,83},{4... | collective-permute-start | bytes 1572872 | tf_op jit(solution)/shard_map/ppermute | solution.py:176
  16.4 53.4 %collective-permute-start.13 = (bf16[4,2,64,512]{3,2,1,0:T(8,128)(2,1)}, bf16[4,2,64,512]{3,2,1,0:T(8,128)(2,1)S(1)}, u32[]{:S(2)}, u32[]{:S(2)}) collective-permute-start(bf16[4,2,64,512]{3,2,1,0:T(8,128)(2,1)} %get-tuple-element.17), channel_id=1, source_target_pairs={{0,512},{64,96},{1,513},{65,97},{2,514},{66,98},{3,515},{67,99},{4... | collective-permute-start | bytes 1572872 | tf_op jit(solution)/shard_map/ppermute | solution.py:176
  21.1 48.8 %collective-permute-start.14 = (bf16[4,2,64,512]{3,2,1,0:T(8,128)(2,1)S(1)}, bf16[4,2,64,512]{3,2,1,0:T(8,128)(2,1)S(1)}, u32[]{:S(2)}, u32[]{:S(2)}) collective-permute-start(bf16[4,2,64,512]{3,2,1,0:T(8,128)(2,1)S(1)} %get-tuple-element.18), channel_id=1, source_target_pairs={{0,768},{64,112},{1,769},{65,113},{2,770},{66,114},{3,771},{67,115... | collective-permute-start | bytes 1572872 | tf_op jit(solution)/shard_map/ppermute | solution.py:176
  26.7 31.1 %collective-permute-start = (bf16[64,512]{1,0:T(8,128)(2,1)S(1)}, bf16[64,512]{1,0:T(8,128)(2,1)S(1)}, u32[]{:S(2)}, u32[]{:S(2)}) collective-permute-start(bf16[64,512]{1,0:T(8,128)(2,1)S(1)} %fusion), channel_id=1, source_target_pairs={{0,136},{64,200},{1,137},{65,201},{2,138},{66,202},{3,139},{67,203... | collective-permute-start | bytes 196616 | tf_op jit(solution)/shard_map/ppermute | solution.py:152
  57.8 20.8 %collective-permute-start.2 = (bf16[2,64,512]{2,1,0:T(8,128)(2,1)S(1)}, bf16[2,64,512]{2,1,0:T(8,128)(2,1)S(1)}, u32[]{:S(2)}, u32[]{:S(2)}) collective-permute-start(bf16[2,64,512]{2,1,0:T(8,128)(2,1)S(1)} %get-tuple-element.24), channel_id=1, source_target_pairs={{0,512},{64,96},{1,513},{65,97},{2,514},{66,98},{3,515},{67,99},{4... | collective-permute-start | bytes 393224 | tf_op jit(solution)/shard_map/ppermute | solution.py:170
  62.8 19.1 %collective-permute-start.1 = (bf16[2,64,512]{2,1,0:T(8,128)(2,1)S(1)}, bf16[2,64,512]{2,1,0:T(8,128)(2,1)S(1)}, u32[]{:S(2)}, u32[]{:S(2)}) collective-permute-start(bf16[2,64,512]{2,1,0:T(8,128)(2,1)S(1)} %get-tuple-element.24), channel_id=1, source_target_pairs={{0,256},{64,80},{1,257},{65,81},{2,258},{66,82},{3,259},{67,83},{4... | collective-permute-start | bytes 393224 | tf_op jit(solution)/shard_map/ppermute | solution.py:170
  65.3 16.6 %collective-permute-start.3 = (bf16[2,64,512]{2,1,0:T(8,128)(2,1)S(1)}, bf16[2,64,512]{2,1,0:T(8,128)(2,1)S(1)}, u32[]{:S(2)}, u32[]{:S(2)}) collective-permute-start(bf16[2,64,512]{2,1,0:T(8,128)(2,1)S(1)} %get-tuple-element.24), channel_id=1, source_target_pairs={{0,768},{64,112},{1,769},{65,113},{2,770},{66,114},{3,771},{67,115... | collective-permute-start | bytes 393224 | tf_op jit(solution)/shard_map/ppermute | solution.py:170
  69.9 0.8 copy-start.5
  70.7 1.0 copy-start.6
  71.7 46.3 %copy-start.2 = (bf16[128,4096]{1,0:T(8,128)(2,1)S(1)}, bf16[128,4096]{1,0:T(8,128)(2,1)}, u32[]{:S(2)}) copy-start(bf16[128,4096]{1,0:T(8,128)(2,1)} %x_ref.5) | copy-start | bytes 3145732
  71.7 46.3 %copy-start.4 = (bf16[128,512]{1,0:T(8,128)(2,1)S(1)}, bf16[128,512]{1,0:T(8,128)(2,1)}, u32[]{:S(2)}) copy-start(bf16[128,512]{1,0:T(8,128)(2,1)} %k_ref.5) | copy-start | bytes 393220
  71.9 17.3 %collective-permute-start.15 = (bf16[2,64,512]{2,1,0:T(8,128)(2,1)S(1)}, bf16[2,64,512]{2,1,0:T(8,128)(2,1)S(1)}, u32[]{:S(2)}, u32[]{:S(2)}) collective-permute-start(bf16[2,64,512]{2,1,0:T(8,128)(2,1)S(1)} %get-tuple-element.20), channel_id=1, source_target_pairs={{0,16},{64,320},{1,17},{65,321},{2,18},{66,322},{3,19},{67,323},{4... | collective-permute-start | bytes 393224 | tf_op jit(solution)/shard_map/ppermute | solution.py:184
  74.8 17.6 %collective-permute-start.16 = (bf16[2,64,512]{2,1,0:T(8,128)(2,1)S(1)}, bf16[2,64,512]{2,1,0:T(8,128)(2,1)S(1)}, u32[]{:S(2)}, u32[]{:S(2)}) collective-permute-start(bf16[2,64,512]{2,1,0:T(8,128)(2,1)S(1)} %get-tuple-element.21), channel_id=1, source_target_pairs={{0,32},{64,576},{1,33},{65,577},{2,34},{66,578},{3,35},{67,579},{4... | collective-permute-start | bytes 393224 | tf_op jit(solution)/shard_map/ppermute | solution.py:184
  78.6 13.8 %collective-permute-start.17 = (bf16[2,64,512]{2,1,0:T(8,128)(2,1)S(1)}, bf16[2,64,512]{2,1,0:T(8,128)(2,1)S(1)}, u32[]{:S(2)}, u32[]{:S(2)}) collective-permute-start(bf16[2,64,512]{2,1,0:T(8,128)(2,1)S(1)} %get-tuple-element.22), channel_id=1, source_target_pairs={{0,48},{64,832},{1,49},{65,833},{2,50},{66,834},{3,51},{67,835},{4... | collective-permute-start | bytes 393224 | tf_op jit(solution)/shard_map/ppermute | solution.py:184
  82.0 27.7 %collective-permute-start.6 = (bf16[4,2,64,512]{3,2,1,0:T(8,128)(2,1)S(1)}, bf16[4,2,64,512]{3,2,1,0:T(8,128)(2,1)S(1)}, u32[]{:S(2)}, u32[]{:S(2)}) collective-permute-start(bf16[4,2,64,512]{3,2,1,0:T(8,128)(2,1)S(1)} %pad_maximum_fusion.refs_0_), channel_id=1, source_target_pairs={{0,48},{64,832},{1,49},{65,833},{2,50},{66,834},{3,51},{67,835},{4... | collective-permute-start | bytes 1572872 | tf_op jit(solution)/shard_map/ppermute | solution.py:178
  84.2 28.0 %collective-permute-start.5 = (bf16[4,2,64,512]{3,2,1,0:T(8,128)(2,1)S(1)}, bf16[4,2,64,512]{3,2,1,0:T(8,128)(2,1)S(1)}, u32[]{:S(2)}, u32[]{:S(2)}) collective-permute-start(bf16[4,2,64,512]{3,2,1,0:T(8,128)(2,1)S(1)} %pad_maximum_fusion.refs_0_), channel_id=1, source_target_pairs={{0,32},{64,576},{1,33},{65,577},{2,34},{66,578},{3,35},{67,579},{4... | collective-permute-start | bytes 1572872 | tf_op jit(solution)/shard_map/ppermute | solution.py:178
  89.2 24.9 %collective-permute-start.4 = (bf16[4,2,64,512]{3,2,1,0:T(8,128)(2,1)S(1)}, bf16[4,2,64,512]{3,2,1,0:T(8,128)(2,1)S(1)}, u32[]{:S(2)}, u32[]{:S(2)}) collective-permute-start(bf16[4,2,64,512]{3,2,1,0:T(8,128)(2,1)S(1)} %pad_maximum_fusion.refs_0_), channel_id=1, source_target_pairs={{0,16},{64,320},{1,17},{65,321},{2,18},{66,322},{3,19},{67,323},{4... | collective-permute-start | bytes 1572872 | tf_op jit(solution)/shard_map/ppermute | solution.py:178
  93.3 41.6 %all-to-all-start = ((bf16[32,16,128]{2,1,0:T(8,128)(2,1)}), bf16[32,16,128]{2,1,0:T(8,128)(2,1)S(1)}, u32[]{:S(2)}, u32[]{:S(2)}) async-start(bf16[32,16,128]{2,1,0:T(8,128)(2,1)} %reshape_reshape.3), calls=%async_computation | async-start | bytes 262144 | tf_op jit(solution)/shard_map/all_to_all | solution.py:189
  107.8 8.7 %collective-permute-start.7 = (bf16[4,2,64,512]{3,2,1,0:T(8,128)(2,1)S(1)}, bf16[4,2,64,512]{3,2,1,0:T(8,128)(2,1)S(1)}, u32[]{:S(2)}, u32[]{:S(2)}) collective-permute-start(bf16[4,2,64,512]{3,2,1,0:T(8,128)(2,1)S(1)} %pad_maximum_fusion.refs_0_), channel_id=1, source_target_pairs={{0,64},{64,0},{1,65},{65,1},{2,66},{66,2},{3,67},{67,3},{4,68},{68... | collective-permute-start | bytes 1572872 | tf_op jit(solution)/shard_map/ppermute | solution.py:185
  109.7 6.8 %collective-permute-start.10 = (bf16[4,2,64,512]{3,2,1,0:T(8,128)(2,1)S(1)}, bf16[4,2,64,512]{3,2,1,0:T(8,128)(2,1)S(1)}, u32[]{:S(2)}, u32[]{:S(2)}) collective-permute-start(bf16[4,2,64,512]{3,2,1,0:T(8,128)(2,1)S(1)} %collective-permute-done.6.refs_3_), channel_id=1, source_target_pairs={{0,64},{64,0},{1,65},{65,1},{2,66},{66,2},{3,67},{67,3},{4,68},{68... | collective-permute-start | bytes 1572872 | tf_op jit(solution)/shard_map/ppermute | solution.py:185
  112.2 4.4 %collective-permute-start.9 = (bf16[4,2,64,512]{3,2,1,0:T(8,128)(2,1)S(1)}, bf16[4,2,64,512]{3,2,1,0:T(8,128)(2,1)S(1)}, u32[]{:S(2)}, u32[]{:S(2)}) collective-permute-start(bf16[4,2,64,512]{3,2,1,0:T(8,128)(2,1)S(1)} %collective-permute-done.5.refs_2_), channel_id=1, source_target_pairs={{0,64},{64,0},{1,65},{65,1},{2,66},{66,2},{3,67},{67,3},{4,68},{68... | collective-permute-start | bytes 1572872 | tf_op jit(solution)/shard_map/ppermute | solution.py:185
  114.1 3.9 %collective-permute-start.8 = (bf16[4,2,64,512]{3,2,1,0:T(8,128)(2,1)S(1)}, bf16[4,2,64,512]{3,2,1,0:T(8,128)(2,1)S(1)}, u32[]{:S(2)}, u32[]{:S(2)}) collective-permute-start(bf16[4,2,64,512]{3,2,1,0:T(8,128)(2,1)S(1)} %collective-permute-done.4.refs_1_), channel_id=1, source_target_pairs={{0,64},{64,0},{1,65},{65,1},{2,66},{66,2},{3,67},{67,3},{4,68},{68... | collective-permute-start | bytes 1572872 | tf_op jit(solution)/shard_map/ppermute | solution.py:185

commit v2 on v1

--- a/solution.py
+++ b/solution.py
@@ -102,29 +102,33 @@
                 ref[j, h] = total.astype(ref.dtype)
 
 
-def split_second_body(own_ref, a_ref, b_ref, c_ref, mine_ref, *out_refs):
+def split_second_body(own_ref, a_ref, b_ref, c_ref, w_ref, v_ref, mine_ref, *out_refs):
     x, y, _, c = coords()
     me = jnp.where(c == 0, y, x)
     for e in range(4):
-        ref = mine_ref if e == 0 else out_refs[e - 1]
         j = up(me, e)
         total = own_ref[j] + a_ref[j].astype(F32) + b_ref[j].astype(F32) + c_ref[j].astype(F32)
-        ref[...] = total.astype(ref.dtype)
-
-
-def project_body(x_ref, k_ref, *refs):
-    pieces, (keys_ref, grad_ref, weight_ref) = refs[:8], refs[8:]
+        if e == 0:
+            mine_ref[...] = total
+        else:
+            out_refs[e - 1][0] = total.astype(BF16)
+            out_refs[e - 1][1, 0] = w_ref[...]
+            out_refs[e - 1][1, 1] = v_ref[...]
+
+
+def project_body(x_ref, k_ref, own_ref, got_ref, keys_ref, grad_ref, weight_ref):
     x, y, zh, c = coords()
     for s in range(2):
         core = c if s == 0 else 1 - c
+        ref = own_ref if s == 0 else got_ref
         for e in range(4):
             for d in range(4):
-                at_x = jnp.where(core == 0, down(x, d), down(x, e))
-                at_y = jnp.where(core == 0, down(y, e), down(y, d))
+                at_x = jnp.where(core == 0, down(x, e), down(x, d))
+                at_y = jnp.where(core == 0, down(y, d), down(y, e))
                 for r in range(2):
                     h = zh if r == 0 else 1 - zh
                     rows = rows_at(((at_x * 2 + h) * 2 + core) * 4 + at_y, 64)
-                    weight_ref[rows, :] = pieces[s * 4 + e][d, r]
+                    weight_ref[rows, :] = ref[e, d, r]
     keys_ref[...] = jnp.dot(x_ref[...], weight_ref[...], preferred_element_type=F32).astype(BF16)
     for b in range(8):
         rows = slice(b * 512, (b + 1) * 512)
@@ -145,10 +149,11 @@
 
 def shards(inputs, weight_codes, code_scales, key_cotangent):
     y = coords()[1]
-    swap = core_swap()
-
-    weight = dequantize(weight_codes, code_scales)
-    quarter = lax.dynamic_slice(weight, (y * 64, 0), (64, 512))
+
+    quarter = dequantize(
+        lax.dynamic_slice(weight_codes, (y * 64, 0), (64, 512)),
+        lax.dynamic_slice(code_scales, (y * 64, 0), (64, 2)),
+    )
     other = lax.ppermute(quarter, BOTH, half_swap())
 
     flops = 2 * 128 * 2048 * 512
@@ -158,7 +163,7 @@
         (inputs, key_cotangent),
         flops=flops,
     )[0]
-    got = lax.ppermute(sent, BOTH, swap)
+    got = lax.ppermute(sent, BOTH, core_swap())
     keep = call(
         functools.partial(term_body, False),
         [shape((2048, 512), F32)],
@@ -166,25 +171,24 @@
         flops=flops,
     )[0]
 
-    base = jnp.stack([quarter, other])
-    line = jnp.stack([base] + [lax.ppermute(base, BOTH, first_axis(d)) for d in (1, 2, 3)])
-
     chunk = (4, 2, 64, 512)
     mine, *outs = call(
         split_first_body, [shape(chunk, F32)] + [shape(chunk, BF16)] * 3, (keep, got)
     )
     ins = [lax.ppermute(o, BOTH, first_axis(d)) for d, o in zip((1, 2, 3), outs)]
 
-    plane = [line] + [lax.ppermute(line, BOTH, second_axis(d)) for d in (1, 2, 3)]
-
-    chunk = (2, 64, 512)
     mine, *outs = call(
-        split_second_body, [shape(chunk, F32)] + [shape(chunk, BF16)] * 3, (mine, *ins)
+        split_second_body,
+        [shape((2, 64, 512), F32)] + [shape((2, 2, 64, 512), BF16)] * 3,
+        (mine, *ins, quarter, other),
     )
     ins = [lax.ppermute(o, BOTH, second_axis(d)) for d, o in zip((1, 2, 3), outs)]
-    swapped = [lax.ppermute(p, BOTH, swap) for p in plane]
-
-    column = mine + sum(i.astype(F32) for i in ins)
+
+    line = jnp.stack([jnp.stack([quarter, other])] + [i[1] for i in ins])
+    plane = jnp.stack([line] + [lax.ppermute(line, BOTH, first_axis(d)) for d in (1, 2, 3)])
+    swapped = lax.ppermute(plane, BOTH, core_swap())
+
+    column = mine + sum(i[0].astype(F32) for i in ins)
     column = column.astype(BF16).reshape(32, 4, 4, 128).reshape(32, 16, 128)
     column = lax.all_to_all(column, BOTH, 0, 0, tiled=True, axis_index_groups=z_groups())
     weight_grad = jnp.sum(column.astype(F32), axis=0).reshape(4, 512)
@@ -192,7 +196,7 @@
     keys, input_grad = call(
         project_body,
         [shape((128, 512), BF16), shape((128, 4096), BF16)],
-        (inputs, key_cotangent, *plane, *swapped),
+        (inputs, key_cotangent, plane, swapped),
         scratch=[pltpu.VMEM((4096, 512), BF16)],
         flops=4 * 128 * 4096 * 512,
     )

time: 138 us -> 153 us (1.11)
  the two profiles are of different devices: /device:TPU:24 before, /device:TPU:1 now
where the time goes in v2:
time: 153 us; the launch traced here: 152 us
  starting transfers between devices  69.8 us (46%)
  blocking collectives  44.8 us (29%)
  waiting for transfers between devices  20.3 us (13%)
  Pallas kernels  10.1 us (7%)
  local copies, waits for them, and re-layouts  5.13 us (3%)
    all_to_all x1, blocking collectives, shards(): lax.all_to_all(column, BOTH, 0, 0, tiled=True, axis_index_groups=z_groups())  44.8 us
    ppermute x3, starting transfers between devices, shards(): lax.ppermute(o, BOTH, second_axis(d))  17.9 us
    ppermute x1, starting transfers between devices, shards(): got = lax.ppermute(sent, BOTH, core_swap())  16.1 us
    ppermute x1, starting transfers between devices, shards(): other = lax.ppermute(quarter, BOTH, half_swap())  12.4 us
    ppermute x3, waiting for transfers between devices, shards(): lax.ppermute(line, BOTH, first_axis(d))  10.6 us
    pallas_call x5, Pallas kernels, call(): pl.pallas_call(body, out_shape=outs, in_specs=[pl.BlockSpec(memory_space=...  10.1 us
    ppermute x3, starting transfers between devices, shards(): lax.ppermute(line, BOTH, first_axis(d))  8.67 us
    ppermute x3, starting transfers between devices, shards(): lax.ppermute(o, BOTH, first_axis(d))  8.4 us
  transfers between devices with their start and end apart: 12, of which 7 were waited for; matrix products, arithmetic and copies ran while one was open for 1% of the time, Pallas kernels for 0%

profile of v2, /device:TPU:1, one launch (start us, length us, event | category | flops | bytes accessed | tf_op | source)
XLA Modules:
  0.0 152.3 jit_solution(4374265504017802912)
XLA Ops:
  0.6 0.0 copy-start
  0.6 0.0 copy-start.2
  0.7 1.2 copy-done.2
  1.9 0.9 copy-done.4
  2.8 0.7 shard_map.68
  3.5 16.1 %collective-permute-start.1 = (bf16[2048,512]{1,0:T(8,128)(2,1)S(1)}, bf16[2048,512]{1,0:T(8,128)(2,1)S(1)}, u32[]{:S(2)}, u32[]{:S(2)}) collective-permute-start(bf16[2048,512]{1,0:T(8,128)(2,1)S(1)} %shard_map.68), channel_id=1, source_target_pairs={{0,64},{64,0},{1,65},{65,1},{2,66},{66,2},{3,67},{67,3},{4,68},{68... | collective-permute-start | bytes 6291464 | tf_op jit(solution)/shard_map/ppermute | solution.py:166
  19.6 0.7 shard_map.67.keep_ref
  20.3 0.0 copy-start.1
  20.3 1.9 %copy-done.1 = f32[2048,512]{1,0:T(8,128)} copy-done((f32[2048,512]{1,0:T(8,128)}, f32[2048,512]{1,0:T(8,128)S(1)}, u32[]{:S(2)}) %copy-start.1) | copy-done | bytes 4194328
  22.3 1.1 collective-permute-done.1.got_ref
  23.4 3.4 %shard_map.69 = (f32[4,2,64,512]{3,2,1,0:T(8,128)S(1)}, bf16[4,2,64,512]{3,2,1,0:T(8,128)(2,1)}, bf16[4,2,64,512]{3,2,1,0:T(8,128)(2,1)}, bf16[4,2,64,512]{3,2,1,0:T(8,128)(2,1)S(1)}) custom-call(f32[2048,512]{1,0:T(8,128)} %copy-done.1, bf16[2048,512]{1,0:T(8,128)(2,1)S(1)} %collective-permute-done.1.got_ref), custom_call_target="tpu_custom_call" | custom-call | bytes 8912896 | tf_op jit(solution)/shard_map/pallas_call | solution.py:71
  26.8 1.9 %collective-permute-start.2 = (bf16[4,2,64,512]{3,2,1,0:T(8,128)(2,1)}, bf16[4,2,64,512]{3,2,1,0:T(8,128)(2,1)S(1)}, u32[]{:S(2)}, u32[]{:S(2)}) collective-permute-start(bf16[4,2,64,512]{3,2,1,0:T(8,128)(2,1)} %get-tuple-element.14), channel_id=1, source_target_pairs={{0,256},{64,80},{1,257},{65,81},{2,258},{66,82},{3,259},{67,83},{4... | collective-permute-start | bytes 1572872 | tf_op jit(solution)/shard_map/ppermute | solution.py:178
  28.7 1.9 %collective-permute-start.3 = (bf16[4,2,64,512]{3,2,1,0:T(8,128)(2,1)}, bf16[4,2,64,512]{3,2,1,0:T(8,128)(2,1)S(1)}, u32[]{:S(2)}, u32[]{:S(2)}) collective-permute-start(bf16[4,2,64,512]{3,2,1,0:T(8,128)(2,1)} %get-tuple-element.15), channel_id=1, source_target_pairs={{0,512},{64,96},{1,513},{65,97},{2,514},{66,98},{3,515},{67,99},{4... | collective-permute-start | bytes 1572872 | tf_op jit(solution)/shard_map/ppermute | solution.py:178
  30.6 4.6 %collective-permute-start.4 = (bf16[4,2,64,512]{3,2,1,0:T(8,128)(2,1)S(1)}, bf16[4,2,64,512]{3,2,1,0:T(8,128)(2,1)S(1)}, u32[]{:S(2)}, u32[]{:S(2)}) collective-permute-start(bf16[4,2,64,512]{3,2,1,0:T(8,128)(2,1)S(1)} %get-tuple-element.16), channel_id=1, source_target_pairs={{0,768},{64,112},{1,769},{65,113},{2,770},{66,114},{3,771},{67,115... | collective-permute-start | bytes 1572872 | tf_op jit(solution)/shard_map/ppermute | solution.py:178
  35.2 0.0 copy-done
  35.2 0.1 constant_dynamic-slice_fusion
  35.3 0.1 copy.7
  35.4 0.1 mul.16
  35.6 0.9 multiply_convert_fusion.w_ref
  36.4 12.4 %collective-permute-start = (bf16[64,512]{1,0:T(8,128)(2,1)S(1)}, bf16[64,512]{1,0:T(8,128)(2,1)S(1)}, u32[]{:S(2)}, u32[]{:S(2)}) collective-permute-start(bf16[64,512]{1,0:T(8,128)(2,1)S(1)} %multiply_convert_fusion.w_ref), channel_id=1, source_target_pairs={{0,136},{64,200},{1,137},{65,201},{2,138},{66,202},{3,139},{67,203... | collective-permute-start | bytes 196616 | tf_op jit(solution)/shard_map/ppermute | solution.py:157
  48.8 2.2 %collective-permute-done.v_ref = bf16[64,512]{1,0:T(8,128)(2,1)S(1)} collective-permute-done((bf16[64,512]{1,0:T(8,128)(2,1)S(1)}, bf16[64,512]{1,0:T(8,128)(2,1)S(1)}, u32[]{:S(2)}, u32[]{:S(2)}) %collective-permute-start) | collective-permute-done | bytes 65568 | tf_op jit(solution)/shard_map/ppermute | solution.py:157
  51.0 0.0 collective-permute-done.2.a_ref
  51.0 0.0 collective-permute-done.3.b_ref
  51.0 0.0 collective-permute-done.4.c_ref
  51.0 0.2 shard_map.70
  51.2 12.7 %collective-permute-start.7 = (bf16[2,2,64,512]{3,2,1,0:T(8,128)(2,1)S(1)}, bf16[2,2,64,512]{3,2,1,0:T(8,128)(2,1)S(1)}, u32[]{:S(2)}, u32[]{:S(2)}) collective-permute-start(bf16[2,2,64,512]{3,2,1,0:T(8,128)(2,1)S(1)} %get-tuple-element.19), channel_id=1, source_target_pairs={{0,48},{64,832},{1,49},{65,833},{2,50},{66,834},{3,51},{67,835},{4... | collective-permute-start | bytes 786440 | tf_op jit(solution)/shard_map/ppermute | solution.py:185
  63.9 2.4 %collective-permute-start.6 = (bf16[2,2,64,512]{3,2,1,0:T(8,128)(2,1)S(1)}, bf16[2,2,64,512]{3,2,1,0:T(8,128)(2,1)S(1)}, u32[]{:S(2)}, u32[]{:S(2)}) collective-permute-start(bf16[2,2,64,512]{3,2,1,0:T(8,128)(2,1)S(1)} %get-tuple-element.18), channel_id=1, source_target_pairs={{0,32},{64,576},{1,33},{65,577},{2,34},{66,578},{3,35},{67,579},{4... | collective-permute-start | bytes 786440 | tf_op jit(solution)/shard_map/ppermute | solution.py:185
  66.4 2.8 %collective-permute-start.5 = (bf16[2,2,64,512]{3,2,1,0:T(8,128)(2,1)S(1)}, bf16[2,2,64,512]{3,2,1,0:T(8,128)(2,1)S(1)}, u32[]{:S(2)}, u32[]{:S(2)}) collective-permute-start(bf16[2,2,64,512]{3,2,1,0:T(8,128)(2,1)S(1)} %get-tuple-element.17), channel_id=1, source_target_pairs={{0,16},{64,320},{1,17},{65,321},{2,18},{66,322},{3,19},{67,323},{4... | collective-permute-start | bytes 786440 | tf_op jit(solution)/shard_map/ppermute | solution.py:185
  69.2 0.0 collective-permute-done.7
  69.2 3.6 %collective-permute-done.6 = bf16[2,2,64,512]{3,2,1,0:T(8,128)(2,1)S(1)} collective-permute-done((bf16[2,2,64,512]{3,2,1,0:T(8,128)(2,1)S(1)}, bf16[2,2,64,512]{3,2,1,0:T(8,128)(2,1)S(1)}, u32[]{:S(2)}, u32[]{:S(2)}) %collective-permute-start.6) | collective-permute-done | bytes 262176 | tf_op jit(solution)/shard_map/ppermute | solution.py:185
  72.8 2.9 %collective-permute-done.5 = bf16[2,2,64,512]{3,2,1,0:T(8,128)(2,1)S(1)} collective-permute-done((bf16[2,2,64,512]{3,2,1,0:T(8,128)(2,1)S(1)}, bf16[2,2,64,512]{3,2,1,0:T(8,128)(2,1)S(1)}, u32[]{:S(2)}, u32[]{:S(2)}) %collective-permute-start.5) | collective-permute-done | bytes 262176 | tf_op jit(solution)/shard_map/ppermute | solution.py:185
  75.7 0.1 fusion.1
  75.8 1.9 %collective-permute-start.10 = (bf16[4,2,64,512]{3,2,1,0:T(8,128)(2,1)S(1)}, bf16[4,2,64,512]{3,2,1,0:T(8,128)(2,1)S(1)}, u32[]{:S(2)}, u32[]{:S(2)}) collective-permute-start(bf16[4,2,64,512]{3,2,1,0:T(8,128)(2,1)S(1)} %get-tuple-element.24), channel_id=1, source_target_pairs={{0,768},{64,112},{1,769},{65,113},{2,770},{66,114},{3,771},{67,115... | collective-permute-start | bytes 1572872 | tf_op jit(solution)/shard_map/ppermute | solution.py:188
  77.7 4.8 %collective-permute-start.9 = (bf16[4,2,64,512]{3,2,1,0:T(8,128)(2,1)S(1)}, bf16[4,2,64,512]{3,2,1,0:T(8,128)(2,1)S(1)}, u32[]{:S(2)}, u32[]{:S(2)}) collective-permute-start(bf16[4,2,64,512]{3,2,1,0:T(8,128)(2,1)S(1)} %get-tuple-element.24), channel_id=1, source_target_pairs={{0,512},{64,96},{1,513},{65,97},{2,514},{66,98},{3,515},{67,99},{4... | collective-permute-start | bytes 1572872 | tf_op jit(solution)/shard_map/ppermute | solution.py:188
  82.5 1.9 %collective-permute-start.8 = (bf16[4,2,64,512]{3,2,1,0:T(8,128)(2,1)S(1)}, bf16[4,2,64,512]{3,2,1,0:T(8,128)(2,1)S(1)}, u32[]{:S(2)}, u32[]{:S(2)}) collective-permute-start(bf16[4,2,64,512]{3,2,1,0:T(8,128)(2,1)S(1)} %get-tuple-element.24), channel_id=1, source_target_pairs={{0,256},{64,80},{1,257},{65,81},{2,258},{66,82},{3,259},{67,83},{4... | collective-permute-start | bytes 1572872 | tf_op jit(solution)/shard_map/ppermute | solution.py:188
  84.5 1.5 %collective-permute-done.10 = bf16[4,2,64,512]{3,2,1,0:T(8,128)(2,1)S(1)} collective-permute-done((bf16[4,2,64,512]{3,2,1,0:T(8,128)(2,1)S(1)}, bf16[4,2,64,512]{3,2,1,0:T(8,128)(2,1)S(1)}, u32[]{:S(2)}, u32[]{:S(2)}) %collective-permute-start.10) | collective-permute-done | bytes 524320 | tf_op jit(solution)/shard_map/ppermute | solution.py:188
  86.0 3.4 %collective-permute-done.9 = bf16[4,2,64,512]{3,2,1,0:T(8,128)(2,1)S(1)} collective-permute-done((bf16[4,2,64,512]{3,2,1,0:T(8,128)(2,1)S(1)}, bf16[4,2,64,512]{3,2,1,0:T(8,128)(2,1)S(1)}, u32[]{:S(2)}, u32[]{:S(2)}) %collective-permute-start.9) | collective-permute-done | bytes 524320 | tf_op jit(solution)/shard_map/ppermute | solution.py:188
  89.4 5.6 %collective-permute-done.8 = bf16[4,2,64,512]{3,2,1,0:T(8,128)(2,1)S(1)} collective-permute-done((bf16[4,2,64,512]{3,2,1,0:T(8,128)(2,1)S(1)}, bf16[4,2,64,512]{3,2,1,0:T(8,128)(2,1)S(1)}, u32[]{:S(2)}, u32[]{:S(2)}) %collective-permute-start.8) | collective-permute-done | bytes 524320 | tf_op jit(solution)/shard_map/ppermute | solution.py:188
  95.0 0.3 pad_maximum_fusion.own_ref
  95.3 6.4 %collective-permute-start.11 = (bf16[4,4,2,64,512]{4,3,2,1,0:T(8,128)(2,1)S(1)}, bf16[4,4,2,64,512]{4,3,2,1,0:T(8,128)(2,1)}, u32[]{:S(2)}, u32[]{:S(2)}) collective-permute-start(bf16[4,4,2,64,512]{4,3,2,1,0:T(8,128)(2,1)S(1)} %pad_maximum_fusion.own_ref), channel_id=1, source_target_pairs={{0,64},{64,0},{1,65},{65,1},{2,66},{66,2},{3,67},{67,3},{4,68},{68... | collective-permute-start | bytes 6291464 | tf_op jit(solution)/shard_map/ppermute | solution.py:189
  101.7 0.1 fusion
  101.8 0.1 reshape_reshape.3
  101.9 44.8 %all_to_all.5 = bf16[32,16,128]{2,1,0:T(8,128)(2,1)S(1)} all-to-all(bf16[32,16,128]{2,1,0:T(8,128)(2,1)S(1)} %reshape_reshape.3), channel_id=1, replica_groups={{0,1,2,3,4,5,6,7,8,9,10,11,12,13,14,15,128,129,130,131,132,133,134,135,..., dimensions={0} | all-to-all | bytes 262144 | tf_op jit(solution)/shard_map/all_to_all | solution.py:193
  146.7 0.6 reshape.18
  147.3 0.0 collective-permute-done.11.got_ref
  147.3 0.0 copy-done.3
  147.3 0.0 copy-done.5
  147.3 5.0 %shard_map.71 = (bf16[128,512]{1,0:T(8,128)(2,1)}, bf16[128,4096]{1,0:T(8,128)(2,1)}) custom-call(bf16[128,4096]{1,0:T(8,128)(2,1)S(1)} %copy-done.3, bf16[128,512]{1,0:T(8,128)(2,1)S(1)} %copy-done.5, bf16[4,4,2,64,512]{4,3,2,1,0:T(8,128)(2,1)S(1)} %pad_maximum_fusion.own_ref, bf16[4,4,2,64,512]{4,3,2,1,0:T(8,128)(2,1)} %collective-permute-done.11.got_ref), custom_call_target="tpu_custom_call" | custom-call | flops 1073741824 | bytes 6553600 | tf_op jit(solution)/shard_map/pallas_call | solution.py:71
  (9 shorter events, 0.1 us)
Async XLA Ops:
  0.6 34.6 %copy-start = (f32[256,2]{0,1:T(2,128)S(1)}, f32[256,2]{0,1:T(2,128)}, u32[]{:S(2)}) copy-start(f32[256,2]{0,1:T(2,128)} %param.6) | copy-start | bytes 6148
  0.6 1.2 copy-start.2
  1.9 0.9 copy-start.4
  3.5 19.8 %collective-permute-start.1 = (bf16[2048,512]{1,0:T(8,128)(2,1)S(1)}, bf16[2048,512]{1,0:T(8,128)(2,1)S(1)}, u32[]{:S(2)}, u32[]{:S(2)}) collective-permute-start(bf16[2048,512]{1,0:T(8,128)(2,1)S(1)} %shard_map.68), channel_id=1, source_target_pairs={{0,64},{64,0},{1,65},{65,1},{2,66},{66,2},{3,67},{67,3},{4,68},{68... | collective-permute-start | bytes 6291464 | tf_op jit(solution)/shard_map/ppermute | solution.py:166
  20.3 2.0 %copy-start.1 = (f32[2048,512]{1,0:T(8,128)}, f32[2048,512]{1,0:T(8,128)S(1)}, u32[]{:S(2)}) copy-start(f32[2048,512]{1,0:T(8,128)S(1)} %shard_map.67.keep_ref) | copy-start | bytes 12582916
  26.8 24.2 %collective-permute-start.2 = (bf16[4,2,64,512]{3,2,1,0:T(8,128)(2,1)}, bf16[4,2,64,512]{3,2,1,0:T(8,128)(2,1)S(1)}, u32[]{:S(2)}, u32[]{:S(2)}) collective-permute-start(bf16[4,2,64,512]{3,2,1,0:T(8,128)(2,1)} %get-tuple-element.14), channel_id=1, source_target_pairs={{0,256},{64,80},{1,257},{65,81},{2,258},{66,82},{3,259},{67,83},{4... | collective-permute-start | bytes 1572872 | tf_op jit(solution)/shard_map/ppermute | solution.py:178
  28.7 22.3 %collective-permute-start.3 = (bf16[4,2,64,512]{3,2,1,0:T(8,128)(2,1)}, bf16[4,2,64,512]{3,2,1,0:T(8,128)(2,1)S(1)}, u32[]{:S(2)}, u32[]{:S(2)}) collective-permute-start(bf16[4,2,64,512]{3,2,1,0:T(8,128)(2,1)} %get-tuple-element.15), channel_id=1, source_target_pairs={{0,512},{64,96},{1,513},{65,97},{2,514},{66,98},{3,515},{67,99},{4... | collective-permute-start | bytes 1572872 | tf_op jit(solution)/shard_map/ppermute | solution.py:178
  30.6 20.3 %collective-permute-start.4 = (bf16[4,2,64,512]{3,2,1,0:T(8,128)(2,1)S(1)}, bf16[4,2,64,512]{3,2,1,0:T(8,128)(2,1)S(1)}, u32[]{:S(2)}, u32[]{:S(2)}) collective-permute-start(bf16[4,2,64,512]{3,2,1,0:T(8,128)(2,1)S(1)} %get-tuple-element.16), channel_id=1, source_target_pairs={{0,768},{64,112},{1,769},{65,113},{2,770},{66,114},{3,771},{67,115... | collective-permute-start | bytes 1572872 | tf_op jit(solution)/shard_map/ppermute | solution.py:178
  36.4 14.5 %collective-permute-start = (bf16[64,512]{1,0:T(8,128)(2,1)S(1)}, bf16[64,512]{1,0:T(8,128)(2,1)S(1)}, u32[]{:S(2)}, u32[]{:S(2)}) collective-permute-start(bf16[64,512]{1,0:T(8,128)(2,1)S(1)} %multiply_convert_fusion.w_ref), channel_id=1, source_target_pairs={{0,136},{64,200},{1,137},{65,201},{2,138},{66,202},{3,139},{67,203... | collective-permute-start | bytes 196616 | tf_op jit(solution)/shard_map/ppermute | solution.py:157
  51.2 17.9 %collective-permute-start.7 = (bf16[2,2,64,512]{3,2,1,0:T(8,128)(2,1)S(1)}, bf16[2,2,64,512]{3,2,1,0:T(8,128)(2,1)S(1)}, u32[]{:S(2)}, u32[]{:S(2)}) collective-permute-start(bf16[2,2,64,512]{3,2,1,0:T(8,128)(2,1)S(1)} %get-tuple-element.19), channel_id=1, source_target_pairs={{0,48},{64,832},{1,49},{65,833},{2,50},{66,834},{3,51},{67,835},{4... | collective-permute-start | bytes 786440 | tf_op jit(solution)/shard_map/ppermute | solution.py:185
  63.9 8.9 %collective-permute-start.6 = (bf16[2,2,64,512]{3,2,1,0:T(8,128)(2,1)S(1)}, bf16[2,2,64,512]{3,2,1,0:T(8,128)(2,1)S(1)}, u32[]{:S(2)}, u32[]{:S(2)}) collective-permute-start(bf16[2,2,64,512]{3,2,1,0:T(8,128)(2,1)S(1)} %get-tuple-element.18), channel_id=1, source_target_pairs={{0,32},{64,576},{1,33},{65,577},{2,34},{66,578},{3,35},{67,579},{4... | collective-permute-start | bytes 786440 | tf_op jit(solution)/shard_map/ppermute | solution.py:185
  66.4 9.3 %collective-permute-start.5 = (bf16[2,2,64,512]{3,2,1,0:T(8,128)(2,1)S(1)}, bf16[2,2,64,512]{3,2,1,0:T(8,128)(2,1)S(1)}, u32[]{:S(2)}, u32[]{:S(2)}) collective-permute-start(bf16[2,2,64,512]{3,2,1,0:T(8,128)(2,1)S(1)} %get-tuple-element.17), channel_id=1, source_target_pairs={{0,16},{64,320},{1,17},{65,321},{2,18},{66,322},{3,19},{67,323},{4... | collective-permute-start | bytes 786440 | tf_op jit(solution)/shard_map/ppermute | solution.py:185
  75.8 10.2 %collective-permute-start.10 = (bf16[4,2,64,512]{3,2,1,0:T(8,128)(2,1)S(1)}, bf16[4,2,64,512]{3,2,1,0:T(8,128)(2,1)S(1)}, u32[]{:S(2)}, u32[]{:S(2)}) collective-permute-start(bf16[4,2,64,512]{3,2,1,0:T(8,128)(2,1)S(1)} %get-tuple-element.24), channel_id=1, source_target_pairs={{0,768},{64,112},{1,769},{65,113},{2,770},{66,114},{3,771},{67,115... | collective-permute-start | bytes 1572872 | tf_op jit(solution)/shard_map/ppermute | solution.py:188
  77.7 11.7 %collective-permute-start.9 = (bf16[4,2,64,512]{3,2,1,0:T(8,128)(2,1)S(1)}, bf16[4,2,64,512]{3,2,1,0:T(8,128)(2,1)S(1)}, u32[]{:S(2)}, u32[]{:S(2)}) collective-permute-start(bf16[4,2,64,512]{3,2,1,0:T(8,128)(2,1)S(1)} %get-tuple-element.24), channel_id=1, source_target_pairs={{0,512},{64,96},{1,513},{65,97},{2,514},{66,98},{3,515},{67,99},{4... | collective-permute-start | bytes 1572872 | tf_op jit(solution)/shard_map/ppermute | solution.py:188
  82.5 12.5 %collective-permute-start.8 = (bf16[4,2,64,512]{3,2,1,0:T(8,128)(2,1)S(1)}, bf16[4,2,64,512]{3,2,1,0:T(8,128)(2,1)S(1)}, u32[]{:S(2)}, u32[]{:S(2)}) collective-permute-start(bf16[4,2,64,512]{3,2,1,0:T(8,128)(2,1)S(1)} %get-tuple-element.24), channel_id=1, source_target_pairs={{0,256},{64,80},{1,257},{65,81},{2,258},{66,82},{3,259},{67,83},{4... | collective-permute-start | bytes 1572872 | tf_op jit(solution)/shard_map/ppermute | solution.py:188
  95.0 52.3 %copy-start.3 = (bf16[128,4096]{1,0:T(8,128)(2,1)S(1)}, bf16[128,4096]{1,0:T(8,128)(2,1)}, u32[]{:S(2)}) copy-start(bf16[128,4096]{1,0:T(8,128)(2,1)} %x_ref.5) | copy-start | bytes 3145732
  95.0 52.3 %copy-start.5 = (bf16[128,512]{1,0:T(8,128)(2,1)S(1)}, bf16[128,512]{1,0:T(8,128)(2,1)}, u32[]{:S(2)}) copy-start(bf16[128,512]{1,0:T(8,128)(2,1)} %k_ref.5) | copy-start | bytes 393220
  95.3 52.0 %collective-permute-start.11 = (bf16[4,4,2,64,512]{4,3,2,1,0:T(8,128)(2,1)S(1)}, bf16[4,4,2,64,512]{4,3,2,1,0:T(8,128)(2,1)}, u32[]{:S(2)}, u32[]{:S(2)}) collective-permute-start(bf16[4,4,2,64,512]{4,3,2,1,0:T(8,128)(2,1)S(1)} %pad_maximum_fusion.own_ref), channel_id=1, source_target_pairs={{0,64},{64,0},{1,65},{65,1},{2,66},{66,2},{3,67},{67,3},{4,68},{68... | collective-permute-start | bytes 6291464 | tf_op jit(solution)/shard_map/ppermute | solution.py:189

commit v3 on v2

--- a/solution.py
+++ b/solution.py
@@ -116,11 +116,11 @@
             out_refs[e - 1][1, 1] = v_ref[...]
 
 
-def project_body(x_ref, k_ref, own_ref, got_ref, keys_ref, grad_ref, weight_ref):
+def project_body(x_ref, k_ref, *refs):
+    pieces, (keys_ref, grad_ref, weight_ref) = refs[:8], refs[8:]
     x, y, zh, c = coords()
     for s in range(2):
         core = c if s == 0 else 1 - c
-        ref = own_ref if s == 0 else got_ref
         for e in range(4):
             for d in range(4):
                 at_x = jnp.where(core == 0, down(x, e), down(x, d))
@@ -128,7 +128,7 @@
                 for r in range(2):
                     h = zh if r == 0 else 1 - zh
                     rows = rows_at(((at_x * 2 + h) * 2 + core) * 4 + at_y, 64)
-                    weight_ref[rows, :] = ref[e, d, r]
+                    weight_ref[rows, :] = pieces[s * 4 + e][d, r]
     keys_ref[...] = jnp.dot(x_ref[...], weight_ref[...], preferred_element_type=F32).astype(BF16)
     for b in range(8):
         rows = slice(b * 512, (b + 1) * 512)
@@ -175,6 +175,7 @@
     mine, *outs = call(
         split_first_body, [shape(chunk, F32)] + [shape(chunk, BF16)] * 3, (keep, got)
     )
+    outs[1], other = lax.optimization_barrier((outs[1], other))
     ins = [lax.ppermute(o, BOTH, first_axis(d)) for d, o in zip((1, 2, 3), outs)]
 
     mine, *outs = call(
@@ -185,18 +186,18 @@
     ins = [lax.ppermute(o, BOTH, second_axis(d)) for d, o in zip((1, 2, 3), outs)]
 
     line = jnp.stack([jnp.stack([quarter, other])] + [i[1] for i in ins])
-    plane = jnp.stack([line] + [lax.ppermute(line, BOTH, first_axis(d)) for d in (1, 2, 3)])
-    swapped = lax.ppermute(plane, BOTH, core_swap())
-
     column = mine + sum(i[0].astype(F32) for i in ins)
     column = column.astype(BF16).reshape(32, 4, 4, 128).reshape(32, 16, 128)
+    plane = [line] + [lax.ppermute(line, BOTH, first_axis(d)) for d in (1, 2, 3)]
+    swapped = [lax.ppermute(p, BOTH, core_swap()) for p in plane]
+
     column = lax.all_to_all(column, BOTH, 0, 0, tiled=True, axis_index_groups=z_groups())
     weight_grad = jnp.sum(column.astype(F32), axis=0).reshape(4, 512)
 
     keys, input_grad = call(
         project_body,
         [shape((128, 512), BF16), shape((128, 4096), BF16)],
-        (inputs, key_cotangent, plane, swapped),
+        (inputs, key_cotangent, *plane, *swapped),
         scratch=[pltpu.VMEM((4096, 512), BF16)],
         flops=4 * 128 * 4096 * 512,
     )

time: 153 us -> 129 us (0.84)
  the two profiles are of different devices: /device:TPU:1 before, /device:TPU:24 now
where the time goes in v3:
time: 129 us; the launch traced here: 128 us
  starting transfers between devices  79.3 us (61%)
  waiting for transfers between devices  30.8 us (24%)
  Pallas kernels  10.4 us (8%)
  local copies, waits for them, and re-layouts  5.77 us (4%)
    ppermute x1, starting transfers between devices, shards(): other = lax.ppermute(quarter, BOTH, half_swap())  23 us
    all_to_all x1, starting transfers between devices, shards(): lax.all_to_all(column, BOTH, 0, 0, tiled=True, axis_index_groups=z_groups())  14.5 us
    ppermute x3, starting transfers between devices, shards(): lax.ppermute(o, BOTH, first_axis(d))  11.4 us
    pallas_call x5, Pallas kernels, call(): pl.pallas_call(body, out_shape=outs, in_specs=[pl.BlockSpec(memory_space=...  10.4 us
    ppermute x3, starting transfers between devices, shards(): lax.ppermute(line, BOTH, first_axis(d))  10.4 us
    ppermute x3, waiting for transfers between devices, shards(): lax.ppermute(o, BOTH, first_axis(d))  10.3 us
    ppermute x3, starting transfers between devices, shards(): lax.ppermute(o, BOTH, second_axis(d))  9.59 us
    ppermute x4, starting transfers between devices, shards(): swapped = [lax.ppermute(p, BOTH, core_swap()) for p in plane]  8.61 us
  transfers between devices with their start and end apart: 16, of which 7 were waited for; matrix products, arithmetic and copies ran while one was open for 2% of the time, Pallas kernels for 3%

profile of v3, /device:TPU:24, one launch (start us, length us, event | category | flops | bytes accessed | tf_op | source)
XLA Modules:
  0.0 128.3 jit_solution(1475274990277809552)
XLA Ops:
  0.6 0.0 copy-start
  0.7 1.2 copy-done.2
  1.9 0.9 copy-done.4
  2.8 2.1 %shard_map.68 = bf16[2048,512]{1,0:T(8,128)(2,1)} custom-call(bf16[128,4096]{1,0:T(8,128)(2,1)S(1)} %copy-done.2, bf16[128,512]{1,0:T(8,128)(2,1)S(1)} %copy-done.4), custom_call_target="tpu_custom_call" | custom-call | flops 268435456 | bytes 3276800 | tf_op jit(solution)/shard_map/pallas_call | solution.py:71
  4.9 1.9 %collective-permute-start = (bf16[2048,512]{1,0:T(8,128)(2,1)}, bf16[2048,512]{1,0:T(8,128)(2,1)S(1)}, u32[]{:S(2)}, u32[]{:S(2)}) collective-permute-start(bf16[2048,512]{1,0:T(8,128)(2,1)} %shard_map.68), channel_id=1, source_target_pairs={{0,64},{64,0},{1,65},{65,1},{2,66},{66,2},{3,67},{67,3},{4,68},{68... | collective-permute-start | bytes 6291464 | tf_op jit(solution)/shard_map/ppermute | solution.py:166
  6.8 0.1 constant_dynamic-slice_fusion
  6.9 0.1 copy.7
  7.0 0.1 mul.16
  7.1 0.9 multiply_convert_fusion.w_ref
  8.0 23.0 %collective-permute-start.1 = (bf16[64,512]{1,0:T(8,128)(2,1)S(1)}, bf16[64,512]{1,0:T(8,128)(2,1)S(1)}, u32[]{:S(2)}, u32[]{:S(2)}) collective-permute-start(bf16[64,512]{1,0:T(8,128)(2,1)S(1)} %multiply_convert_fusion.w_ref), channel_id=1, source_target_pairs={{0,136},{64,200},{1,137},{65,201},{2,138},{66,202},{3,139},{67,203... | collective-permute-start | bytes 196616 | tf_op jit(solution)/shard_map/ppermute | solution.py:157
  31.0 0.7 shard_map.67.keep_ref
  31.8 1.9 %copy-done.1 = f32[2048,512]{1,0:T(8,128)} copy-done((f32[2048,512]{1,0:T(8,128)}, f32[2048,512]{1,0:T(8,128)S(1)}, u32[]{:S(2)}) %copy-start.1) | copy-done | bytes 4194328
  33.7 0.0 collective-permute-done.got_ref
  33.7 2.5 %shard_map.69 = (f32[4,2,64,512]{3,2,1,0:T(8,128)S(1)}, bf16[4,2,64,512]{3,2,1,0:T(8,128)(2,1)S(1)}, bf16[4,2,64,512]{3,2,1,0:T(8,128)(2,1)S(1)}, bf16[4,2,64,512]{3,2,1,0:T(8,128)(2,1)S(1)}) custom-call(f32[2048,512]{1,0:T(8,128)} %copy-done.1, bf16[2048,512]{1,0:T(8,128)(2,1)S(1)} %collective-permute-done.got_ref), custom_call_target="tpu_custom_call" | custom-call | bytes 8912896 | tf_op jit(solution)/shard_map/pallas_call | solution.py:71
  36.2 3.4 %collective-permute-start.2 = (bf16[4,2,64,512]{3,2,1,0:T(8,128)(2,1)S(1)}, bf16[4,2,64,512]{3,2,1,0:T(8,128)(2,1)S(1)}, u32[]{:S(2)}, u32[]{:S(2)}) collective-permute-start(bf16[4,2,64,512]{3,2,1,0:T(8,128)(2,1)S(1)} %get-tuple-element.18), channel_id=1, source_target_pairs={{0,256},{64,80},{1,257},{65,81},{2,258},{66,82},{3,259},{67,83},{4... | collective-permute-start | bytes 1572872 | tf_op jit(solution)/shard_map/ppermute | solution.py:179
  39.6 3.2 %collective-permute-done.1.v_ref = bf16[64,512]{1,0:T(8,128)(2,1)S(1)} collective-permute-done((bf16[64,512]{1,0:T(8,128)(2,1)S(1)}, bf16[64,512]{1,0:T(8,128)(2,1)S(1)}, u32[]{:S(2)}, u32[]{:S(2)}) %collective-permute-start.1) | collective-permute-done | bytes 65568 | tf_op jit(solution)/shard_map/ppermute | solution.py:157
  42.9 4.9 %collective-permute-start.3 = (bf16[4,2,64,512]{3,2,1,0:T(8,128)(2,1)S(1)}, bf16[4,2,64,512]{3,2,1,0:T(8,128)(2,1)S(1)}, u32[]{:S(2)}, u32[]{:S(2)}) collective-permute-start(bf16[4,2,64,512]{3,2,1,0:T(8,128)(2,1)S(1)} %get-tuple-element.19), channel_id=1, source_target_pairs={{0,512},{64,96},{1,513},{65,97},{2,514},{66,98},{3,515},{67,99},{4... | collective-permute-start | bytes 1572872 | tf_op jit(solution)/shard_map/ppermute | solution.py:179
  47.8 3.0 %collective-permute-start.4 = (bf16[4,2,64,512]{3,2,1,0:T(8,128)(2,1)S(1)}, bf16[4,2,64,512]{3,2,1,0:T(8,128)(2,1)S(1)}, u32[]{:S(2)}, u32[]{:S(2)}) collective-permute-start(bf16[4,2,64,512]{3,2,1,0:T(8,128)(2,1)S(1)} %get-tuple-element.20), channel_id=1, source_target_pairs={{0,768},{64,112},{1,769},{65,113},{2,770},{66,114},{3,771},{67,115... | collective-permute-start | bytes 1572872 | tf_op jit(solution)/shard_map/ppermute | solution.py:179
  50.8 0.0 collective-permute-done.2.a_ref
  50.9 4.6 %collective-permute-done.3.b_ref = bf16[4,2,64,512]{3,2,1,0:T(8,128)(2,1)S(1)} collective-permute-done((bf16[4,2,64,512]{3,2,1,0:T(8,128)(2,1)S(1)}, bf16[4,2,64,512]{3,2,1,0:T(8,128)(2,1)S(1)}, u32[]{:S(2)}, u32[]{:S(2)}) %collective-permute-start.3) | collective-permute-done | bytes 524320 | tf_op jit(solution)/shard_map/ppermute | solution.py:179
  55.4 5.7 %collective-permute-done.4.c_ref = bf16[4,2,64,512]{3,2,1,0:T(8,128)(2,1)S(1)} collective-permute-done((bf16[4,2,64,512]{3,2,1,0:T(8,128)(2,1)S(1)}, bf16[4,2,64,512]{3,2,1,0:T(8,128)(2,1)S(1)}, u32[]{:S(2)}, u32[]{:S(2)}) %collective-permute-start.4) | collective-permute-done | bytes 524320 | tf_op jit(solution)/shard_map/ppermute | solution.py:179
  61.2 0.2 shard_map.70
  61.4 2.7 %collective-permute-start.7 = (bf16[2,2,64,512]{3,2,1,0:T(8,128)(2,1)S(1)}, bf16[2,2,64,512]{3,2,1,0:T(8,128)(2,1)S(1)}, u32[]{:S(2)}, u32[]{:S(2)}) collective-permute-start(bf16[2,2,64,512]{3,2,1,0:T(8,128)(2,1)S(1)} %get-tuple-element.23), channel_id=1, source_target_pairs={{0,48},{64,832},{1,49},{65,833},{2,50},{66,834},{3,51},{67,835},{4... | collective-permute-start | bytes 786440 | tf_op jit(solution)/shard_map/ppermute | solution.py:186
  64.1 2.8 %collective-permute-start.6 = (bf16[2,2,64,512]{3,2,1,0:T(8,128)(2,1)S(1)}, bf16[2,2,64,512]{3,2,1,0:T(8,128)(2,1)S(1)}, u32[]{:S(2)}, u32[]{:S(2)}) collective-permute-start(bf16[2,2,64,512]{3,2,1,0:T(8,128)(2,1)S(1)} %get-tuple-element.22), channel_id=1, source_target_pairs={{0,32},{64,576},{1,33},{65,577},{2,34},{66,578},{3,35},{67,579},{4... | collective-permute-start | bytes 786440 | tf_op jit(solution)/shard_map/ppermute | solution.py:186
  66.9 4.1 %collective-permute-start.5 = (bf16[2,2,64,512]{3,2,1,0:T(8,128)(2,1)S(1)}, bf16[2,2,64,512]{3,2,1,0:T(8,128)(2,1)S(1)}, u32[]{:S(2)}, u32[]{:S(2)}) collective-permute-start(bf16[2,2,64,512]{3,2,1,0:T(8,128)(2,1)S(1)} %get-tuple-element.21), channel_id=1, source_target_pairs={{0,16},{64,320},{1,17},{65,321},{2,18},{66,322},{3,19},{67,323},{4... | collective-permute-start | bytes 786440 | tf_op jit(solution)/shard_map/ppermute | solution.py:186
  71.0 0.0 collective-permute-done.7
  71.1 2.8 %collective-permute-done.6 = bf16[2,2,64,512]{3,2,1,0:T(8,128)(2,1)S(1)} collective-permute-done((bf16[2,2,64,512]{3,2,1,0:T(8,128)(2,1)S(1)}, bf16[2,2,64,512]{3,2,1,0:T(8,128)(2,1)S(1)}, u32[]{:S(2)}, u32[]{:S(2)}) %collective-permute-start.6) | collective-permute-done | bytes 262176 | tf_op jit(solution)/shard_map/ppermute | solution.py:186
  73.8 2.6 %collective-permute-done.5 = bf16[2,2,64,512]{3,2,1,0:T(8,128)(2,1)S(1)} collective-permute-done((bf16[2,2,64,512]{3,2,1,0:T(8,128)(2,1)S(1)}, bf16[2,2,64,512]{3,2,1,0:T(8,128)(2,1)S(1)}, u32[]{:S(2)}, u32[]{:S(2)}) %collective-permute-start.5) | collective-permute-done | bytes 262176 | tf_op jit(solution)/shard_map/ppermute | solution.py:186
  76.5 0.1 fusion
  76.5 0.7 reshape_reshape.3
  77.3 14.5 %all-to-all-start = ((bf16[32,16,128]{2,1,0:T(8,128)(2,1)}), bf16[32,16,128]{2,1,0:T(8,128)(2,1)S(1)}, u32[]{:S(2)}, u32[]{:S(2)}) async-start(bf16[32,16,128]{2,1,0:T(8,128)(2,1)} %reshape_reshape.3), calls=%async_computation | async-start | bytes 262144 | tf_op jit(solution)/shard_map/all_to_all | solution.py:194
  91.8 0.1 pad_maximum_fusion.refs_0_
  91.9 3.3 %collective-permute-start.8 = (bf16[4,2,64,512]{3,2,1,0:T(8,128)(2,1)S(1)}, bf16[4,2,64,512]{3,2,1,0:T(8,128)(2,1)S(1)}, u32[]{:S(2)}, u32[]{:S(2)}) collective-permute-start(bf16[4,2,64,512]{3,2,1,0:T(8,128)(2,1)S(1)} %pad_maximum_fusion.refs_0_), channel_id=1, source_target_pairs={{0,256},{64,80},{1,257},{65,81},{2,258},{66,82},{3,259},{67,83},{4... | collective-permute-start | bytes 1572872 | tf_op jit(solution)/shard_map/ppermute | solution.py:191
  95.2 4.6 %collective-permute-start.9 = (bf16[4,2,64,512]{3,2,1,0:T(8,128)(2,1)S(1)}, bf16[4,2,64,512]{3,2,1,0:T(8,128)(2,1)S(1)}, u32[]{:S(2)}, u32[]{:S(2)}) collective-permute-start(bf16[4,2,64,512]{3,2,1,0:T(8,128)(2,1)S(1)} %pad_maximum_fusion.refs_0_), channel_id=1, source_target_pairs={{0,512},{64,96},{1,513},{65,97},{2,514},{66,98},{3,515},{67,99},{4... | collective-permute-start | bytes 1572872 | tf_op jit(solution)/shard_map/ppermute | solution.py:191
  99.8 2.5 %collective-permute-start.10 = (bf16[4,2,64,512]{3,2,1,0:T(8,128)(2,1)S(1)}, bf16[4,2,64,512]{3,2,1,0:T(8,128)(2,1)S(1)}, u32[]{:S(2)}, u32[]{:S(2)}) collective-permute-start(bf16[4,2,64,512]{3,2,1,0:T(8,128)(2,1)S(1)} %pad_maximum_fusion.refs_0_), channel_id=1, source_target_pairs={{0,768},{64,112},{1,769},{65,113},{2,770},{66,114},{3,771},{67,115... | collective-permute-start | bytes 1572872 | tf_op jit(solution)/shard_map/ppermute | solution.py:191
  102.3 1.9 %collective-permute-start.11 = (bf16[4,2,64,512]{3,2,1,0:T(8,128)(2,1)S(1)}, bf16[4,2,64,512]{3,2,1,0:T(8,128)(2,1)}, u32[]{:S(2)}, u32[]{:S(2)}) collective-permute-start(bf16[4,2,64,512]{3,2,1,0:T(8,128)(2,1)S(1)} %pad_maximum_fusion.refs_0_), channel_id=1, source_target_pairs={{0,64},{64,0},{1,65},{65,1},{2,66},{66,2},{3,67},{67,3},{4,68},{68... | collective-permute-start | bytes 1572872 | tf_op jit(solution)/shard_map/ppermute | solution.py:192
  104.2 0.0 collective-permute-done.8.refs_1_
  104.2 2.4 %collective-permute-start.12 = (bf16[4,2,64,512]{3,2,1,0:T(8,128)(2,1)S(1)}, bf16[4,2,64,512]{3,2,1,0:T(8,128)(2,1)}, u32[]{:S(2)}, u32[]{:S(2)}) collective-permute-start(bf16[4,2,64,512]{3,2,1,0:T(8,128)(2,1)S(1)} %collective-permute-done.8.refs_1_), channel_id=1, source_target_pairs={{0,64},{64,0},{1,65},{65,1},{2,66},{66,2},{3,67},{67,3},{4,68},{68... | collective-permute-start | bytes 1572872 | tf_op jit(solution)/shard_map/ppermute | solution.py:192
  106.6 4.0 %collective-permute-done.9.refs_2_ = bf16[4,2,64,512]{3,2,1,0:T(8,128)(2,1)S(1)} collective-permute-done((bf16[4,2,64,512]{3,2,1,0:T(8,128)(2,1)S(1)}, bf16[4,2,64,512]{3,2,1,0:T(8,128)(2,1)S(1)}, u32[]{:S(2)}, u32[]{:S(2)}) %collective-permute-start.9) | collective-permute-done | bytes 524320 | tf_op jit(solution)/shard_map/ppermute | solution.py:191
  110.7 1.9 %collective-permute-start.13 = (bf16[4,2,64,512]{3,2,1,0:T(8,128)(2,1)S(1)}, bf16[4,2,64,512]{3,2,1,0:T(8,128)(2,1)}, u32[]{:S(2)}, u32[]{:S(2)}) collective-permute-start(bf16[4,2,64,512]{3,2,1,0:T(8,128)(2,1)S(1)} %collective-permute-done.9.refs_2_), channel_id=1, source_target_pairs={{0,64},{64,0},{1,65},{65,1},{2,66},{66,2},{3,67},{67,3},{4,68},{68... | collective-permute-start | bytes 1572872 | tf_op jit(solution)/shard_map/ppermute | solution.py:192
  112.6 0.0 collective-permute-done.10.refs_3_
  112.6 2.4 %collective-permute-start.14 = (bf16[4,2,64,512]{3,2,1,0:T(8,128)(2,1)S(1)}, bf16[4,2,64,512]{3,2,1,0:T(8,128)(2,1)}, u32[]{:S(2)}, u32[]{:S(2)}) collective-permute-start(bf16[4,2,64,512]{3,2,1,0:T(8,128)(2,1)S(1)} %collective-permute-done.10.refs_3_), channel_id=1, source_target_pairs={{0,64},{64,0},{1,65},{65,1},{2,66},{66,2},{3,67},{67,3},{4,68},{68... | collective-permute-start | bytes 1572872 | tf_op jit(solution)/shard_map/ppermute | solution.py:192
  115.0 7.7 %all-to-all-done = bf16[32,16,128]{2,1,0:T(8,128)(2,1)S(1)} async-done(((bf16[32,16,128]{2,1,0:T(8,128)(2,1)}), bf16[32,16,128]{2,1,0:T(8,128)(2,1)S(1)}, u32[]{:S(2)}, u32[]{:S(2)}) %all-to-all-start) | async-done | bytes 131104 | tf_op jit(solution)/shard_map/all_to_all | solution.py:194
  122.8 0.6 reshape.18
  123.4 0.0 collective-permute-done.11.refs_4_
  123.4 0.0 collective-permute-done.13.refs_6_
  123.4 0.0 collective-permute-done.14.refs_7_
  123.4 4.9 %shard_map.71 = (bf16[128,512]{1,0:T(8,128)(2,1)}, bf16[128,4096]{1,0:T(8,128)(2,1)}) custom-call(bf16[128,4096]{1,0:T(8,128)(2,1)S(1)} %copy-done.3, bf16[128,512]{1,0:T(8,128)(2,1)S(1)} %copy-done.5, bf16[4,2,64,512]{3,2,1,0:T(8,128)(2,1)S(1)} %pad_maximum_fusion.refs_0_, bf16[4,2,64,512]{3,2,1,0:T(8,128)(2,1)S(1)} %collective-permute-done.8.refs_1_, ...), custom_call_target="tpu_custom_call" | custom-call | flops 1073741824 | bytes 6553600 | tf_op jit(solution)/shard_map/pallas_call | solution.py:71
  (15 shorter events, 0.1 us)
Async XLA Ops:
  0.6 6.2 %copy-start = (f32[256,2]{0,1:T(2,128)S(1)}, f32[256,2]{0,1:T(2,128)}, u32[]{:S(2)}) copy-start(f32[256,2]{0,1:T(2,128)} %param.6) | copy-start | bytes 6148
  0.6 1.2 copy-start.2
  1.9 0.9 copy-start.4
  2.8 28.2 %copy-start.3 = (bf16[128,4096]{1,0:T(8,128)(2,1)S(1)}, bf16[128,4096]{1,0:T(8,128)(2,1)}, u32[]{:S(2)}) copy-start(bf16[128,4096]{1,0:T(8,128)(2,1)} %x_ref.5) | copy-start | bytes 3145732
  2.8 28.2 %copy-start.5 = (bf16[128,512]{1,0:T(8,128)(2,1)S(1)}, bf16[128,512]{1,0:T(8,128)(2,1)}, u32[]{:S(2)}) copy-start(bf16[128,512]{1,0:T(8,128)(2,1)} %k_ref.5) | copy-start | bytes 393220
  4.9 28.8 %collective-permute-start = (bf16[2048,512]{1,0:T(8,128)(2,1)}, bf16[2048,512]{1,0:T(8,128)(2,1)S(1)}, u32[]{:S(2)}, u32[]{:S(2)}) collective-permute-start(bf16[2048,512]{1,0:T(8,128)(2,1)} %shard_map.68), channel_id=1, source_target_pairs={{0,64},{64,0},{1,65},{65,1},{2,66},{66,2},{3,67},{67,3},{4,68},{68... | collective-permute-start | bytes 6291464 | tf_op jit(solution)/shard_map/ppermute | solution.py:166
  8.0 34.9 %collective-permute-start.1 = (bf16[64,512]{1,0:T(8,128)(2,1)S(1)}, bf16[64,512]{1,0:T(8,128)(2,1)S(1)}, u32[]{:S(2)}, u32[]{:S(2)}) collective-permute-start(bf16[64,512]{1,0:T(8,128)(2,1)S(1)} %multiply_convert_fusion.w_ref), channel_id=1, source_target_pairs={{0,136},{64,200},{1,137},{65,201},{2,138},{66,202},{3,139},{67,203... | collective-permute-start | bytes 196616 | tf_op jit(solution)/shard_map/ppermute | solution.py:157
  31.8 1.9 %copy-start.1 = (f32[2048,512]{1,0:T(8,128)}, f32[2048,512]{1,0:T(8,128)S(1)}, u32[]{:S(2)}) copy-start(f32[2048,512]{1,0:T(8,128)S(1)} %shard_map.67.keep_ref) | copy-start | bytes 12582916
  36.2 14.6 %collective-permute-start.2 = (bf16[4,2,64,512]{3,2,1,0:T(8,128)(2,1)S(1)}, bf16[4,2,64,512]{3,2,1,0:T(8,128)(2,1)S(1)}, u32[]{:S(2)}, u32[]{:S(2)}) collective-permute-start(bf16[4,2,64,512]{3,2,1,0:T(8,128)(2,1)S(1)} %get-tuple-element.18), channel_id=1, source_target_pairs={{0,256},{64,80},{1,257},{65,81},{2,258},{66,82},{3,259},{67,83},{4... | collective-permute-start | bytes 1572872 | tf_op jit(solution)/shard_map/ppermute | solution.py:179
  42.9 12.6 %collective-permute-start.3 = (bf16[4,2,64,512]{3,2,1,0:T(8,128)(2,1)S(1)}, bf16[4,2,64,512]{3,2,1,0:T(8,128)(2,1)S(1)}, u32[]{:S(2)}, u32[]{:S(2)}) collective-permute-start(bf16[4,2,64,512]{3,2,1,0:T(8,128)(2,1)S(1)} %get-tuple-element.19), channel_id=1, source_target_pairs={{0,512},{64,96},{1,513},{65,97},{2,514},{66,98},{3,515},{67,99},{4... | collective-permute-start | bytes 1572872 | tf_op jit(solution)/shard_map/ppermute | solution.py:179
  47.8 13.4 %collective-permute-start.4 = (bf16[4,2,64,512]{3,2,1,0:T(8,128)(2,1)S(1)}, bf16[4,2,64,512]{3,2,1,0:T(8,128)(2,1)S(1)}, u32[]{:S(2)}, u32[]{:S(2)}) collective-permute-start(bf16[4,2,64,512]{3,2,1,0:T(8,128)(2,1)S(1)} %get-tuple-element.20), channel_id=1, source_target_pairs={{0,768},{64,112},{1,769},{65,113},{2,770},{66,114},{3,771},{67,115... | collective-permute-start | bytes 1572872 | tf_op jit(solution)/shard_map/ppermute | solution.py:179
  61.4 9.6 %collective-permute-start.7 = (bf16[2,2,64,512]{3,2,1,0:T(8,128)(2,1)S(1)}, bf16[2,2,64,512]{3,2,1,0:T(8,128)(2,1)S(1)}, u32[]{:S(2)}, u32[]{:S(2)}) collective-permute-start(bf16[2,2,64,512]{3,2,1,0:T(8,128)(2,1)S(1)} %get-tuple-element.23), channel_id=1, source_target_pairs={{0,48},{64,832},{1,49},{65,833},{2,50},{66,834},{3,51},{67,835},{4... | collective-permute-start | bytes 786440 | tf_op jit(solution)/shard_map/ppermute | solution.py:186
  64.1 9.8 %collective-permute-start.6 = (bf16[2,2,64,512]{3,2,1,0:T(8,128)(2,1)S(1)}, bf16[2,2,64,512]{3,2,1,0:T(8,128)(2,1)S(1)}, u32[]{:S(2)}, u32[]{:S(2)}) collective-permute-start(bf16[2,2,64,512]{3,2,1,0:T(8,128)(2,1)S(1)} %get-tuple-element.22), channel_id=1, source_target_pairs={{0,32},{64,576},{1,33},{65,577},{2,34},{66,578},{3,35},{67,579},{4... | collective-permute-start | bytes 786440 | tf_op jit(solution)/shard_map/ppermute | solution.py:186
  66.9 9.5 %collective-permute-start.5 = (bf16[2,2,64,512]{3,2,1,0:T(8,128)(2,1)S(1)}, bf16[2,2,64,512]{3,2,1,0:T(8,128)(2,1)S(1)}, u32[]{:S(2)}, u32[]{:S(2)}) collective-permute-start(bf16[2,2,64,512]{3,2,1,0:T(8,128)(2,1)S(1)} %get-tuple-element.21), channel_id=1, source_target_pairs={{0,16},{64,320},{1,17},{65,321},{2,18},{66,322},{3,19},{67,323},{4... | collective-permute-start | bytes 786440 | tf_op jit(solution)/shard_map/ppermute | solution.py:186
  77.3 45.5 %all-to-all-start = ((bf16[32,16,128]{2,1,0:T(8,128)(2,1)}), bf16[32,16,128]{2,1,0:T(8,128)(2,1)S(1)}, u32[]{:S(2)}, u32[]{:S(2)}) async-start(bf16[32,16,128]{2,1,0:T(8,128)(2,1)} %reshape_reshape.3), calls=%async_computation | async-start | bytes 262144 | tf_op jit(solution)/shard_map/all_to_all | solution.py:194
  91.9 12.3 %collective-permute-start.8 = (bf16[4,2,64,512]{3,2,1,0:T(8,128)(2,1)S(1)}, bf16[4,2,64,512]{3,2,1,0:T(8,128)(2,1)S(1)}, u32[]{:S(2)}, u32[]{:S(2)}) collective-permute-start(bf16[4,2,64,512]{3,2,1,0:T(8,128)(2,1)S(1)} %pad_maximum_fusion.refs_0_), channel_id=1, source_target_pairs={{0,256},{64,80},{1,257},{65,81},{2,258},{66,82},{3,259},{67,83},{4... | collective-permute-start | bytes 1572872 | tf_op jit(solution)/shard_map/ppermute | solution.py:191
  95.2 15.5 %collective-permute-start.9 = (bf16[4,2,64,512]{3,2,1,0:T(8,128)(2,1)S(1)}, bf16[4,2,64,512]{3,2,1,0:T(8,128)(2,1)S(1)}, u32[]{:S(2)}, u32[]{:S(2)}) collective-permute-start(bf16[4,2,64,512]{3,2,1,0:T(8,128)(2,1)S(1)} %pad_maximum_fusion.refs_0_), channel_id=1, source_target_pairs={{0,512},{64,96},{1,513},{65,97},{2,514},{66,98},{3,515},{67,99},{4... | collective-permute-start | bytes 1572872 | tf_op jit(solution)/shard_map/ppermute | solution.py:191
  99.8 12.8 %collective-permute-start.10 = (bf16[4,2,64,512]{3,2,1,0:T(8,128)(2,1)S(1)}, bf16[4,2,64,512]{3,2,1,0:T(8,128)(2,1)S(1)}, u32[]{:S(2)}, u32[]{:S(2)}) collective-permute-start(bf16[4,2,64,512]{3,2,1,0:T(8,128)(2,1)S(1)} %pad_maximum_fusion.refs_0_), channel_id=1, source_target_pairs={{0,768},{64,112},{1,769},{65,113},{2,770},{66,114},{3,771},{67,115... | collective-permute-start | bytes 1572872 | tf_op jit(solution)/shard_map/ppermute | solution.py:191
  102.3 21.1 %collective-permute-start.11 = (bf16[4,2,64,512]{3,2,1,0:T(8,128)(2,1)S(1)}, bf16[4,2,64,512]{3,2,1,0:T(8,128)(2,1)}, u32[]{:S(2)}, u32[]{:S(2)}) collective-permute-start(bf16[4,2,64,512]{3,2,1,0:T(8,128)(2,1)S(1)} %pad_maximum_fusion.refs_0_), channel_id=1, source_target_pairs={{0,64},{64,0},{1,65},{65,1},{2,66},{66,2},{3,67},{67,3},{4,68},{68... | collective-permute-start | bytes 1572872 | tf_op jit(solution)/shard_map/ppermute | solution.py:192
  104.2 19.2 %collective-permute-start.12 = (bf16[4,2,64,512]{3,2,1,0:T(8,128)(2,1)S(1)}, bf16[4,2,64,512]{3,2,1,0:T(8,128)(2,1)}, u32[]{:S(2)}, u32[]{:S(2)}) collective-permute-start(bf16[4,2,64,512]{3,2,1,0:T(8,128)(2,1)S(1)} %collective-permute-done.8.refs_1_), channel_id=1, source_target_pairs={{0,64},{64,0},{1,65},{65,1},{2,66},{66,2},{3,67},{67,3},{4,68},{68... | collective-permute-start | bytes 1572872 | tf_op jit(solution)/shard_map/ppermute | solution.py:192
  110.7 12.7 %collective-permute-start.13 = (bf16[4,2,64,512]{3,2,1,0:T(8,128)(2,1)S(1)}, bf16[4,2,64,512]{3,2,1,0:T(8,128)(2,1)}, u32[]{:S(2)}, u32[]{:S(2)}) collective-permute-start(bf16[4,2,64,512]{3,2,1,0:T(8,128)(2,1)S(1)} %collective-permute-done.9.refs_2_), channel_id=1, source_target_pairs={{0,64},{64,0},{1,65},{65,1},{2,66},{66,2},{3,67},{67,3},{4,68},{68... | collective-permute-start | bytes 1572872 | tf_op jit(solution)/shard_map/ppermute | solution.py:192
  112.6 10.8 %collective-permute-start.14 = (bf16[4,2,64,512]{3,2,1,0:T(8,128)(2,1)S(1)}, bf16[4,2,64,512]{3,2,1,0:T(8,128)(2,1)}, u32[]{:S(2)}, u32[]{:S(2)}) collective-permute-start(bf16[4,2,64,512]{3,2,1,0:T(8,128)(2,1)S(1)} %collective-permute-done.10.refs_3_), channel_id=1, source_target_pairs={{0,64},{64,0},{1,65},{65,1},{2,66},{66,2},{3,67},{67,3},{4,68},{68... | collective-permute-start | bytes 1572872 | tf_op jit(solution)/shard_map/ppermute | solution.py:192

commit v4 on v3

--- a/solution.py
+++ b/solution.py
@@ -102,18 +102,14 @@
                 ref[j, h] = total.astype(ref.dtype)
 
 
-def split_second_body(own_ref, a_ref, b_ref, c_ref, w_ref, v_ref, mine_ref, *out_refs):
+def split_second_body(own_ref, a_ref, b_ref, c_ref, mine_ref, *out_refs):
     x, y, _, c = coords()
     me = jnp.where(c == 0, y, x)
     for e in range(4):
+        ref = mine_ref if e == 0 else out_refs[e - 1]
         j = up(me, e)
         total = own_ref[j] + a_ref[j].astype(F32) + b_ref[j].astype(F32) + c_ref[j].astype(F32)
-        if e == 0:
-            mine_ref[...] = total
-        else:
-            out_refs[e - 1][0] = total.astype(BF16)
-            out_refs[e - 1][1, 0] = w_ref[...]
-            out_refs[e - 1][1, 1] = v_ref[...]
+        ref[...] = total.astype(ref.dtype)
 
 
 def project_body(x_ref, k_ref, *refs):
@@ -166,7 +162,7 @@
     got = lax.ppermute(sent, BOTH, core_swap())
     keep = call(
         functools.partial(term_body, False),
-        [shape((2048, 512), F32)],
+        [shape((2048, 512), BF16)],
         (inputs, key_cotangent),
         flops=flops,
     )[0]
@@ -175,19 +171,20 @@
     mine, *outs = call(
         split_first_body, [shape(chunk, F32)] + [shape(chunk, BF16)] * 3, (keep, got)
     )
-    outs[1], other = lax.optimization_barrier((outs[1], other))
     ins = [lax.ppermute(o, BOTH, first_axis(d)) for d, o in zip((1, 2, 3), outs)]
 
     mine, *outs = call(
         split_second_body,
-        [shape((2, 64, 512), F32)] + [shape((2, 2, 64, 512), BF16)] * 3,
-        (mine, *ins, quarter, other),
+        [shape((2, 64, 512), F32)] + [shape((2, 64, 512), BF16)] * 3,
+        (mine, *ins),
     )
     ins = [lax.ppermute(o, BOTH, second_axis(d)) for d, o in zip((1, 2, 3), outs)]
 
-    line = jnp.stack([jnp.stack([quarter, other])] + [i[1] for i in ins])
-    column = mine + sum(i[0].astype(F32) for i in ins)
+    column = mine + sum(i.astype(F32) for i in ins)
     column = column.astype(BF16).reshape(32, 4, 4, 128).reshape(32, 16, 128)
+    base = jnp.stack([quarter, other])
+    base, column = lax.optimization_barrier((base, column))
+    line = jnp.stack([base] + [lax.ppermute(base, BOTH, second_axis(d)) for d in (1, 2, 3)])
     plane = [line] + [lax.ppermute(line, BOTH, first_axis(d)) for d in (1, 2, 3)]
     swapped = [lax.ppermute(p, BOTH, core_swap()) for p in plane]
 

time: 129 us -> 127 us (0.984)
  the two profiles are of different devices: /device:TPU:24 before, /device:TPU:10 now
where the time goes in v4:
time: 127 us; the launch traced here: 126 us
  starting transfers between devices  91.7 us (72%)
  waiting for transfers between devices  16.2 us (13%)
  Pallas kernels  9.54 us (8%)
  local copies, waits for them, and re-layouts  6.98 us (5%)
    ppermute x1, starting transfers between devices, shards(): other = lax.ppermute(quarter, BOTH, half_swap())  23 us
    all_to_all x1, starting transfers between devices, shards(): lax.all_to_all(column, BOTH, 0, 0, tiled=True, axis_index_groups=z_groups())  15.8 us
    ppermute x3, starting transfers between devices, shards(): lax.ppermute(base, BOTH, second_axis(d))  12.1 us
    ppermute x3, starting transfers between devices, shards(): lax.ppermute(o, BOTH, second_axis(d))  10.8 us
    ppermute x3, starting transfers between devices, shards(): lax.ppermute(o, BOTH, first_axis(d))  10.5 us
    pallas_call x5, Pallas kernels, call(): pl.pallas_call(body, out_shape=outs, in_specs=[pl.BlockSpec(memory_space=...  9.54 us
    ppermute x3, starting transfers between devices, shards(): lax.ppermute(line, BOTH, first_axis(d))  9.46 us
    ppermute x4, starting transfers between devices, shards(): swapped = [lax.ppermute(p, BOTH, core_swap()) for p in plane]  8.15 us
  transfers between devices with their start and end apart: 19, of which 6 were waited for; matrix products, arithmetic and copies ran while one was open for 2% of the time, Pallas kernels for 1%

profile of v4, /device:TPU:10, one launch (start us, length us, event | category | flops | bytes accessed | tf_op | source)
XLA Modules:
  0.0 126.4 jit_solution(1355927626132721476)
XLA Ops:
  0.6 0.0 copy-start
  0.6 0.0 copy-start.1
  0.7 1.2 copy-done.1
  1.9 0.9 copy-done.3
  2.8 0.7 shard_map.68
  3.5 1.9 %collective-permute-start.1 = (bf16[2048,512]{1,0:T(8,128)(2,1)S(1)}, bf16[2048,512]{1,0:T(8,128)(2,1)S(1)}, u32[]{:S(2)}, u32[]{:S(2)}) collective-permute-start(bf16[2048,512]{1,0:T(8,128)(2,1)S(1)} %shard_map.68), channel_id=1, source_target_pairs={{0,64},{64,0},{1,65},{65,1},{2,66},{66,2},{3,67},{67,3},{4,68},{68... | collective-permute-start | bytes 6291464 | tf_op jit(solution)/shard_map/ppermute | solution.py:162
  5.5 0.7 shard_map.67.keep_ref
  6.2 3.4 %collective-permute-done.1.got_ref = bf16[2048,512]{1,0:T(8,128)(2,1)S(1)} collective-permute-done((bf16[2048,512]{1,0:T(8,128)(2,1)S(1)}, bf16[2048,512]{1,0:T(8,128)(2,1)S(1)}, u32[]{:S(2)}, u32[]{:S(2)}) %collective-permute-start.1) | collective-permute-done | bytes 2097184 | tf_op jit(solution)/shard_map/ppermute | solution.py:162
  9.6 1.3 %copy-done.7 = bf16[2048,512]{1,0:T(8,128)(2,1)} copy-done((bf16[2048,512]{1,0:T(8,128)(2,1)}, bf16[2048,512]{1,0:T(8,128)(2,1)S(1)}, u32[]{:S(2)}) %copy-start.7) | copy-done | bytes 2097176
  10.9 3.0 %shard_map.69 = (f32[4,2,64,512]{3,2,1,0:T(8,128)S(1)}, bf16[4,2,64,512]{3,2,1,0:T(8,128)(2,1)}, bf16[4,2,64,512]{3,2,1,0:T(8,128)(2,1)}, bf16[4,2,64,512]{3,2,1,0:T(8,128)(2,1)S(1)}) custom-call(bf16[2048,512]{1,0:T(8,128)(2,1)S(1)} %shard_map.67.keep_ref, bf16[2048,512]{1,0:T(8,128)(2,1)} %copy-done.7), custom_call_target="tpu_custom_call" | custom-call | bytes 6815744 | tf_op jit(solution)/shard_map/pallas_call | solution.py:71
  13.9 3.4 %collective-permute-start.2 = (bf16[4,2,64,512]{3,2,1,0:T(8,128)(2,1)}, bf16[4,2,64,512]{3,2,1,0:T(8,128)(2,1)S(1)}, u32[]{:S(2)}, u32[]{:S(2)}) collective-permute-start(bf16[4,2,64,512]{3,2,1,0:T(8,128)(2,1)} %get-tuple-element.16), channel_id=1, source_target_pairs={{0,256},{64,80},{1,257},{65,81},{2,258},{66,82},{3,259},{67,83},{4... | collective-permute-start | bytes 1572872 | tf_op jit(solution)/shard_map/ppermute | solution.py:174
  17.3 3.0 %collective-permute-start.3 = (bf16[4,2,64,512]{3,2,1,0:T(8,128)(2,1)}, bf16[4,2,64,512]{3,2,1,0:T(8,128)(2,1)S(1)}, u32[]{:S(2)}, u32[]{:S(2)}) collective-permute-start(bf16[4,2,64,512]{3,2,1,0:T(8,128)(2,1)} %get-tuple-element.17), channel_id=1, source_target_pairs={{0,512},{64,96},{1,513},{65,97},{2,514},{66,98},{3,515},{67,99},{4... | collective-permute-start | bytes 1572872 | tf_op jit(solution)/shard_map/ppermute | solution.py:174
  20.3 4.1 %collective-permute-start.4 = (bf16[4,2,64,512]{3,2,1,0:T(8,128)(2,1)S(1)}, bf16[4,2,64,512]{3,2,1,0:T(8,128)(2,1)S(1)}, u32[]{:S(2)}, u32[]{:S(2)}) collective-permute-start(bf16[4,2,64,512]{3,2,1,0:T(8,128)(2,1)S(1)} %get-tuple-element.18), channel_id=1, source_target_pairs={{0,768},{64,112},{1,769},{65,113},{2,770},{66,114},{3,771},{67,115... | collective-permute-start | bytes 1572872 | tf_op jit(solution)/shard_map/ppermute | solution.py:174
  24.4 0.1 constant_dynamic-slice_fusion
  24.5 0.1 copy.7
  24.6 0.1 mul.16
  24.7 0.9 multiply_convert_fusion
  25.6 23.0 %collective-permute-start = (bf16[64,512]{1,0:T(8,128)(2,1)S(1)}, bf16[64,512]{1,0:T(8,128)(2,1)S(1)}, u32[]{:S(2)}, u32[]{:S(2)}) collective-permute-start(bf16[64,512]{1,0:T(8,128)(2,1)S(1)} %multiply_convert_fusion), channel_id=1, source_target_pairs={{0,136},{64,200},{1,137},{65,201},{2,138},{66,202},{3,139},{67,203... | collective-permute-start | bytes 196616 | tf_op jit(solution)/shard_map/ppermute | solution.py:153
  48.6 0.0 collective-permute-done.3.b_ref
  48.6 0.0 collective-permute-done.4.c_ref
  48.6 0.0 copy-start.5
  48.6 0.8 copy-done.5
  49.4 1.0 copy-done.6
  50.5 0.2 shard_map.70
  50.7 3.6 %collective-permute-start.5 = (bf16[2,64,512]{2,1,0:T(8,128)(2,1)S(1)}, bf16[2,64,512]{2,1,0:T(8,128)(2,1)S(1)}, u32[]{:S(2)}, u32[]{:S(2)}) collective-permute-start(bf16[2,64,512]{2,1,0:T(8,128)(2,1)S(1)} %get-tuple-element.20), channel_id=1, source_target_pairs={{0,16},{64,320},{1,17},{65,321},{2,18},{66,322},{3,19},{67,323},{4... | collective-permute-start | bytes 393224 | tf_op jit(solution)/shard_map/ppermute | solution.py:181
  54.3 2.9 %collective-permute-start.6 = (bf16[2,64,512]{2,1,0:T(8,128)(2,1)S(1)}, bf16[2,64,512]{2,1,0:T(8,128)(2,1)S(1)}, u32[]{:S(2)}, u32[]{:S(2)}) collective-permute-start(bf16[2,64,512]{2,1,0:T(8,128)(2,1)S(1)} %get-tuple-element.21), channel_id=1, source_target_pairs={{0,32},{64,576},{1,33},{65,577},{2,34},{66,578},{3,35},{67,579},{4... | collective-permute-start | bytes 393224 | tf_op jit(solution)/shard_map/ppermute | solution.py:181
  57.2 4.3 %collective-permute-start.7 = (bf16[2,64,512]{2,1,0:T(8,128)(2,1)S(1)}, bf16[2,64,512]{2,1,0:T(8,128)(2,1)S(1)}, u32[]{:S(2)}, u32[]{:S(2)}) collective-permute-start(bf16[2,64,512]{2,1,0:T(8,128)(2,1)S(1)} %get-tuple-element.22), channel_id=1, source_target_pairs={{0,48},{64,832},{1,49},{65,833},{2,50},{66,834},{3,51},{67,835},{4... | collective-permute-start | bytes 393224 | tf_op jit(solution)/shard_map/ppermute | solution.py:181
  61.5 1.1 collective-permute-done.6
  62.7 1.4 %collective-permute-done.7 = bf16[2,64,512]{2,1,0:T(8,128)(2,1)S(1)} collective-permute-done((bf16[2,64,512]{2,1,0:T(8,128)(2,1)S(1)}, bf16[2,64,512]{2,1,0:T(8,128)(2,1)S(1)}, u32[]{:S(2)}, u32[]{:S(2)}) %collective-permute-start.7) | collective-permute-done | bytes 131104 | tf_op jit(solution)/shard_map/ppermute | solution.py:181
  64.1 0.1 add_convert_fusion
  64.2 0.7 reshape_reshape.3
  64.9 4.3 %collective-permute-start.10 = (bf16[2,64,512]{2,1,0:T(8,128)(2,1)S(1)}, bf16[2,64,512]{2,1,0:T(8,128)(2,1)S(1)}, u32[]{:S(2)}, u32[]{:S(2)}) collective-permute-start(bf16[2,64,512]{2,1,0:T(8,128)(2,1)S(1)} %pad_maximum_fusion.1), channel_id=1, source_target_pairs={{0,48},{64,832},{1,49},{65,833},{2,50},{66,834},{3,51},{67,835},{4... | collective-permute-start | bytes 393224 | tf_op jit(solution)/shard_map/ppermute | solution.py:187
  69.2 3.3 %collective-permute-start.9 = (bf16[2,64,512]{2,1,0:T(8,128)(2,1)S(1)}, bf16[2,64,512]{2,1,0:T(8,128)(2,1)S(1)}, u32[]{:S(2)}, u32[]{:S(2)}) collective-permute-start(bf16[2,64,512]{2,1,0:T(8,128)(2,1)S(1)} %pad_maximum_fusion.1), channel_id=1, source_target_pairs={{0,32},{64,576},{1,33},{65,577},{2,34},{66,578},{3,35},{67,579},{4... | collective-permute-start | bytes 393224 | tf_op jit(solution)/shard_map/ppermute | solution.py:187
  72.5 4.5 %collective-permute-start.8 = (bf16[2,64,512]{2,1,0:T(8,128)(2,1)S(1)}, bf16[2,64,512]{2,1,0:T(8,128)(2,1)S(1)}, u32[]{:S(2)}, u32[]{:S(2)}) collective-permute-start(bf16[2,64,512]{2,1,0:T(8,128)(2,1)S(1)} %pad_maximum_fusion.1), channel_id=1, source_target_pairs={{0,16},{64,320},{1,17},{65,321},{2,18},{66,322},{3,19},{67,323},{4... | collective-permute-start | bytes 393224 | tf_op jit(solution)/shard_map/ppermute | solution.py:187
  77.0 15.8 %all-to-all-start = ((bf16[32,16,128]{2,1,0:T(8,128)(2,1)}), bf16[32,16,128]{2,1,0:T(8,128)(2,1)S(1)}, u32[]{:S(2)}, u32[]{:S(2)}) async-start(bf16[32,16,128]{2,1,0:T(8,128)(2,1)} %reshape_reshape.3), calls=%async_computation | async-start | bytes 262144 | tf_op jit(solution)/shard_map/all_to_all | solution.py:191
  92.9 0.1 pad_maximum_fusion.refs_0_
  92.9 1.9 %collective-permute-start.13 = (bf16[4,2,64,512]{3,2,1,0:T(8,128)(2,1)S(1)}, bf16[4,2,64,512]{3,2,1,0:T(8,128)(2,1)S(1)}, u32[]{:S(2)}, u32[]{:S(2)}) collective-permute-start(bf16[4,2,64,512]{3,2,1,0:T(8,128)(2,1)S(1)} %pad_maximum_fusion.refs_0_), channel_id=1, source_target_pairs={{0,768},{64,112},{1,769},{65,113},{2,770},{66,114},{3,771},{67,115... | collective-permute-start | bytes 1572872 | tf_op jit(solution)/shard_map/ppermute | solution.py:188
  94.9 4.0 %collective-permute-start.12 = (bf16[4,2,64,512]{3,2,1,0:T(8,128)(2,1)S(1)}, bf16[4,2,64,512]{3,2,1,0:T(8,128)(2,1)S(1)}, u32[]{:S(2)}, u32[]{:S(2)}) collective-permute-start(bf16[4,2,64,512]{3,2,1,0:T(8,128)(2,1)S(1)} %pad_maximum_fusion.refs_0_), channel_id=1, source_target_pairs={{0,512},{64,96},{1,513},{65,97},{2,514},{66,98},{3,515},{67,99},{4... | collective-permute-start | bytes 1572872 | tf_op jit(solution)/shard_map/ppermute | solution.py:188
  98.8 3.6 %collective-permute-start.11 = (bf16[4,2,64,512]{3,2,1,0:T(8,128)(2,1)S(1)}, bf16[4,2,64,512]{3,2,1,0:T(8,128)(2,1)S(1)}, u32[]{:S(2)}, u32[]{:S(2)}) collective-permute-start(bf16[4,2,64,512]{3,2,1,0:T(8,128)(2,1)S(1)} %pad_maximum_fusion.refs_0_), channel_id=1, source_target_pairs={{0,256},{64,80},{1,257},{65,81},{2,258},{66,82},{3,259},{67,83},{4... | collective-permute-start | bytes 1572872 | tf_op jit(solution)/shard_map/ppermute | solution.py:188
  102.4 1.9 %collective-permute-start.14 = (bf16[4,2,64,512]{3,2,1,0:T(8,128)(2,1)S(1)}, bf16[4,2,64,512]{3,2,1,0:T(8,128)(2,1)}, u32[]{:S(2)}, u32[]{:S(2)}) collective-permute-start(bf16[4,2,64,512]{3,2,1,0:T(8,128)(2,1)S(1)} %pad_maximum_fusion.refs_0_), channel_id=1, source_target_pairs={{0,64},{64,0},{1,65},{65,1},{2,66},{66,2},{3,67},{67,3},{4,68},{68... | collective-permute-start | bytes 1572872 | tf_op jit(solution)/shard_map/ppermute | solution.py:189
  104.4 2.4 %collective-permute-start.17 = (bf16[4,2,64,512]{3,2,1,0:T(8,128)(2,1)S(1)}, bf16[4,2,64,512]{3,2,1,0:T(8,128)(2,1)}, u32[]{:S(2)}, u32[]{:S(2)}) collective-permute-start(bf16[4,2,64,512]{3,2,1,0:T(8,128)(2,1)S(1)} %collective-permute-done.13.refs_3_), channel_id=1, source_target_pairs={{0,64},{64,0},{1,65},{65,1},{2,66},{66,2},{3,67},{67,3},{4,68},{68... | collective-permute-start | bytes 1572872 | tf_op jit(solution)/shard_map/ppermute | solution.py:189
  106.8 2.9 %collective-permute-done.12.refs_2_ = bf16[4,2,64,512]{3,2,1,0:T(8,128)(2,1)S(1)} collective-permute-done((bf16[4,2,64,512]{3,2,1,0:T(8,128)(2,1)S(1)}, bf16[4,2,64,512]{3,2,1,0:T(8,128)(2,1)S(1)}, u32[]{:S(2)}, u32[]{:S(2)}) %collective-permute-start.12) | collective-permute-done | bytes 524320 | tf_op jit(solution)/shard_map/ppermute | solution.py:188
  109.7 1.9 %collective-permute-start.16 = (bf16[4,2,64,512]{3,2,1,0:T(8,128)(2,1)S(1)}, bf16[4,2,64,512]{3,2,1,0:T(8,128)(2,1)}, u32[]{:S(2)}, u32[]{:S(2)}) collective-permute-start(bf16[4,2,64,512]{3,2,1,0:T(8,128)(2,1)S(1)} %collective-permute-done.12.refs_2_), channel_id=1, source_target_pairs={{0,64},{64,0},{1,65},{65,1},{2,66},{66,2},{3,67},{67,3},{4,68},{68... | collective-permute-start | bytes 1572872 | tf_op jit(solution)/shard_map/ppermute | solution.py:189
  111.6 2.1 %collective-permute-done.11.refs_1_ = bf16[4,2,64,512]{3,2,1,0:T(8,128)(2,1)S(1)} collective-permute-done((bf16[4,2,64,512]{3,2,1,0:T(8,128)(2,1)S(1)}, bf16[4,2,64,512]{3,2,1,0:T(8,128)(2,1)S(1)}, u32[]{:S(2)}, u32[]{:S(2)}) %collective-permute-start.11) | collective-permute-done | bytes 524320 | tf_op jit(solution)/shard_map/ppermute | solution.py:188
  113.7 1.9 %collective-permute-start.15 = (bf16[4,2,64,512]{3,2,1,0:T(8,128)(2,1)S(1)}, bf16[4,2,64,512]{3,2,1,0:T(8,128)(2,1)}, u32[]{:S(2)}, u32[]{:S(2)}) collective-permute-start(bf16[4,2,64,512]{3,2,1,0:T(8,128)(2,1)S(1)} %collective-permute-done.11.refs_1_), channel_id=1, source_target_pairs={{0,64},{64,0},{1,65},{65,1},{2,66},{66,2},{3,67},{67,3},{4,68},{68... | collective-permute-start | bytes 1572872 | tf_op jit(solution)/shard_map/ppermute | solution.py:189
  115.6 5.2 %all-to-all-done = bf16[32,16,128]{2,1,0:T(8,128)(2,1)S(1)} async-done(((bf16[32,16,128]{2,1,0:T(8,128)(2,1)}), bf16[32,16,128]{2,1,0:T(8,128)(2,1)S(1)}, u32[]{:S(2)}, u32[]{:S(2)}) %all-to-all-start) | async-done | bytes 131104 | tf_op jit(solution)/shard_map/all_to_all | solution.py:191
  120.9 0.6 reshape.13
  121.5 4.9 %shard_map.71 = (bf16[128,512]{1,0:T(8,128)(2,1)}, bf16[128,4096]{1,0:T(8,128)(2,1)}) custom-call(bf16[128,4096]{1,0:T(8,128)(2,1)S(1)} %copy-done.2, bf16[128,512]{1,0:T(8,128)(2,1)S(1)} %copy-done.4, bf16[4,2,64,512]{3,2,1,0:T(8,128)(2,1)S(1)} %pad_maximum_fusion.refs_0_, bf16[4,2,64,512]{3,2,1,0:T(8,128)(2,1)S(1)} %collective-permute-done.11.refs_1_, ...), custom_call_target="tpu_custom_call" | custom-call | flops 1073741824 | bytes 6553600 | tf_op jit(solution)/shard_map/pallas_call | solution.py:71
  (22 shorter events, 0.1 us)
Async XLA Ops:
  0.6 23.8 %copy-start = (f32[256,2]{0,1:T(2,128)S(1)}, f32[256,2]{0,1:T(2,128)}, u32[]{:S(2)}) copy-start(f32[256,2]{0,1:T(2,128)} %param.6) | copy-start | bytes 6148
  0.6 1.2 copy-start.1
  1.9 0.9 copy-start.3
  3.5 6.1 %collective-permute-start.1 = (bf16[2048,512]{1,0:T(8,128)(2,1)S(1)}, bf16[2048,512]{1,0:T(8,128)(2,1)S(1)}, u32[]{:S(2)}, u32[]{:S(2)}) collective-permute-start(bf16[2048,512]{1,0:T(8,128)(2,1)S(1)} %shard_map.68), channel_id=1, source_target_pairs={{0,64},{64,0},{1,65},{65,1},{2,66},{66,2},{3,67},{67,3},{4,68},{68... | collective-permute-start | bytes 6291464 | tf_op jit(solution)/shard_map/ppermute | solution.py:162
  9.6 1.3 %copy-start.7 = (bf16[2048,512]{1,0:T(8,128)(2,1)}, bf16[2048,512]{1,0:T(8,128)(2,1)S(1)}, u32[]{:S(2)}) copy-start(bf16[2048,512]{1,0:T(8,128)(2,1)S(1)} %collective-permute-done.1.got_ref) | copy-start | bytes 6291460
  13.9 34.7 %collective-permute-start.2 = (bf16[4,2,64,512]{3,2,1,0:T(8,128)(2,1)}, bf16[4,2,64,512]{3,2,1,0:T(8,128)(2,1)S(1)}, u32[]{:S(2)}, u32[]{:S(2)}) collective-permute-start(bf16[4,2,64,512]{3,2,1,0:T(8,128)(2,1)} %get-tuple-element.16), channel_id=1, source_target_pairs={{0,256},{64,80},{1,257},{65,81},{2,258},{66,82},{3,259},{67,83},{4... | collective-permute-start | bytes 1572872 | tf_op jit(solution)/shard_map/ppermute | solution.py:174
  17.3 31.3 %collective-permute-start.3 = (bf16[4,2,64,512]{3,2,1,0:T(8,128)(2,1)}, bf16[4,2,64,512]{3,2,1,0:T(8,128)(2,1)S(1)}, u32[]{:S(2)}, u32[]{:S(2)}) collective-permute-start(bf16[4,2,64,512]{3,2,1,0:T(8,128)(2,1)} %get-tuple-element.17), channel_id=1, source_target_pairs={{0,512},{64,96},{1,513},{65,97},{2,514},{66,98},{3,515},{67,99},{4... | collective-permute-start | bytes 1572872 | tf_op jit(solution)/shard_map/ppermute | solution.py:174
  20.3 28.3 %collective-permute-start.4 = (bf16[4,2,64,512]{3,2,1,0:T(8,128)(2,1)S(1)}, bf16[4,2,64,512]{3,2,1,0:T(8,128)(2,1)S(1)}, u32[]{:S(2)}, u32[]{:S(2)}) collective-permute-start(bf16[4,2,64,512]{3,2,1,0:T(8,128)(2,1)S(1)} %get-tuple-element.18), channel_id=1, source_target_pairs={{0,768},{64,112},{1,769},{65,113},{2,770},{66,114},{3,771},{67,115... | collective-permute-start | bytes 1572872 | tf_op jit(solution)/shard_map/ppermute | solution.py:174
  25.6 35.9 %collective-permute-start = (bf16[64,512]{1,0:T(8,128)(2,1)S(1)}, bf16[64,512]{1,0:T(8,128)(2,1)S(1)}, u32[]{:S(2)}, u32[]{:S(2)}) collective-permute-start(bf16[64,512]{1,0:T(8,128)(2,1)S(1)} %multiply_convert_fusion), channel_id=1, source_target_pairs={{0,136},{64,200},{1,137},{65,201},{2,138},{66,202},{3,139},{67,203... | collective-permute-start | bytes 196616 | tf_op jit(solution)/shard_map/ppermute | solution.py:153
  48.6 0.8 copy-start.5
  49.4 1.0 copy-start.6
  50.5 71.0 %copy-start.2 = (bf16[128,4096]{1,0:T(8,128)(2,1)S(1)}, bf16[128,4096]{1,0:T(8,128)(2,1)}, u32[]{:S(2)}) copy-start(bf16[128,4096]{1,0:T(8,128)(2,1)} %x_ref.5) | copy-start | bytes 3145732
  50.5 71.0 %copy-start.4 = (bf16[128,512]{1,0:T(8,128)(2,1)S(1)}, bf16[128,512]{1,0:T(8,128)(2,1)}, u32[]{:S(2)}) copy-start(bf16[128,512]{1,0:T(8,128)(2,1)} %k_ref.5) | copy-start | bytes 393220
  50.7 10.8 %collective-permute-start.5 = (bf16[2,64,512]{2,1,0:T(8,128)(2,1)S(1)}, bf16[2,64,512]{2,1,0:T(8,128)(2,1)S(1)}, u32[]{:S(2)}, u32[]{:S(2)}) collective-permute-start(bf16[2,64,512]{2,1,0:T(8,128)(2,1)S(1)} %get-tuple-element.20), channel_id=1, source_target_pairs={{0,16},{64,320},{1,17},{65,321},{2,18},{66,322},{3,19},{67,323},{4... | collective-permute-start | bytes 393224 | tf_op jit(solution)/shard_map/ppermute | solution.py:181
  54.3 8.4 %collective-permute-start.6 = (bf16[2,64,512]{2,1,0:T(8,128)(2,1)S(1)}, bf16[2,64,512]{2,1,0:T(8,128)(2,1)S(1)}, u32[]{:S(2)}, u32[]{:S(2)}) collective-permute-start(bf16[2,64,512]{2,1,0:T(8,128)(2,1)S(1)} %get-tuple-element.21), channel_id=1, source_target_pairs={{0,32},{64,576},{1,33},{65,577},{2,34},{66,578},{3,35},{67,579},{4... | collective-permute-start | bytes 393224 | tf_op jit(solution)/shard_map/ppermute | solution.py:181
  57.2 6.9 %collective-permute-start.7 = (bf16[2,64,512]{2,1,0:T(8,128)(2,1)S(1)}, bf16[2,64,512]{2,1,0:T(8,128)(2,1)S(1)}, u32[]{:S(2)}, u32[]{:S(2)}) collective-permute-start(bf16[2,64,512]{2,1,0:T(8,128)(2,1)S(1)} %get-tuple-element.22), channel_id=1, source_target_pairs={{0,48},{64,832},{1,49},{65,833},{2,50},{66,834},{3,51},{67,835},{4... | collective-permute-start | bytes 393224 | tf_op jit(solution)/shard_map/ppermute | solution.py:181
  64.9 27.9 %collective-permute-start.10 = (bf16[2,64,512]{2,1,0:T(8,128)(2,1)S(1)}, bf16[2,64,512]{2,1,0:T(8,128)(2,1)S(1)}, u32[]{:S(2)}, u32[]{:S(2)}) collective-permute-start(bf16[2,64,512]{2,1,0:T(8,128)(2,1)S(1)} %pad_maximum_fusion.1), channel_id=1, source_target_pairs={{0,48},{64,832},{1,49},{65,833},{2,50},{66,834},{3,51},{67,835},{4... | collective-permute-start | bytes 393224 | tf_op jit(solution)/shard_map/ppermute | solution.py:187
  69.2 23.7 %collective-permute-start.9 = (bf16[2,64,512]{2,1,0:T(8,128)(2,1)S(1)}, bf16[2,64,512]{2,1,0:T(8,128)(2,1)S(1)}, u32[]{:S(2)}, u32[]{:S(2)}) collective-permute-start(bf16[2,64,512]{2,1,0:T(8,128)(2,1)S(1)} %pad_maximum_fusion.1), channel_id=1, source_target_pairs={{0,32},{64,576},{1,33},{65,577},{2,34},{66,578},{3,35},{67,579},{4... | collective-permute-start | bytes 393224 | tf_op jit(solution)/shard_map/ppermute | solution.py:187
  72.5 20.4 %collective-permute-start.8 = (bf16[2,64,512]{2,1,0:T(8,128)(2,1)S(1)}, bf16[2,64,512]{2,1,0:T(8,128)(2,1)S(1)}, u32[]{:S(2)}, u32[]{:S(2)}) collective-permute-start(bf16[2,64,512]{2,1,0:T(8,128)(2,1)S(1)} %pad_maximum_fusion.1), channel_id=1, source_target_pairs={{0,16},{64,320},{1,17},{65,321},{2,18},{66,322},{3,19},{67,323},{4... | collective-permute-start | bytes 393224 | tf_op jit(solution)/shard_map/ppermute | solution.py:187
  77.0 43.8 %all-to-all-start = ((bf16[32,16,128]{2,1,0:T(8,128)(2,1)}), bf16[32,16,128]{2,1,0:T(8,128)(2,1)S(1)}, u32[]{:S(2)}, u32[]{:S(2)}) async-start(bf16[32,16,128]{2,1,0:T(8,128)(2,1)} %reshape_reshape.3), calls=%async_computation | async-start | bytes 262144 | tf_op jit(solution)/shard_map/all_to_all | solution.py:191
  92.9 11.4 %collective-permute-start.13 = (bf16[4,2,64,512]{3,2,1,0:T(8,128)(2,1)S(1)}, bf16[4,2,64,512]{3,2,1,0:T(8,128)(2,1)S(1)}, u32[]{:S(2)}, u32[]{:S(2)}) collective-permute-start(bf16[4,2,64,512]{3,2,1,0:T(8,128)(2,1)S(1)} %pad_maximum_fusion.refs_0_), channel_id=1, source_target_pairs={{0,768},{64,112},{1,769},{65,113},{2,770},{66,114},{3,771},{67,115... | collective-permute-start | bytes 1572872 | tf_op jit(solution)/shard_map/ppermute | solution.py:188
  94.9 14.8 %collective-permute-start.12 = (bf16[4,2,64,512]{3,2,1,0:T(8,128)(2,1)S(1)}, bf16[4,2,64,512]{3,2,1,0:T(8,128)(2,1)S(1)}, u32[]{:S(2)}, u32[]{:S(2)}) collective-permute-start(bf16[4,2,64,512]{3,2,1,0:T(8,128)(2,1)S(1)} %pad_maximum_fusion.refs_0_), channel_id=1, source_target_pairs={{0,512},{64,96},{1,513},{65,97},{2,514},{66,98},{3,515},{67,99},{4... | collective-permute-start | bytes 1572872 | tf_op jit(solution)/shard_map/ppermute | solution.py:188
  98.8 14.8 %collective-permute-start.11 = (bf16[4,2,64,512]{3,2,1,0:T(8,128)(2,1)S(1)}, bf16[4,2,64,512]{3,2,1,0:T(8,128)(2,1)S(1)}, u32[]{:S(2)}, u32[]{:S(2)}) collective-permute-start(bf16[4,2,64,512]{3,2,1,0:T(8,128)(2,1)S(1)} %pad_maximum_fusion.refs_0_), channel_id=1, source_target_pairs={{0,256},{64,80},{1,257},{65,81},{2,258},{66,82},{3,259},{67,83},{4... | collective-permute-start | bytes 1572872 | tf_op jit(solution)/shard_map/ppermute | solution.py:188
  102.4 19.0 %collective-permute-start.14 = (bf16[4,2,64,512]{3,2,1,0:T(8,128)(2,1)S(1)}, bf16[4,2,64,512]{3,2,1,0:T(8,128)(2,1)}, u32[]{:S(2)}, u32[]{:S(2)}) collective-permute-start(bf16[4,2,64,512]{3,2,1,0:T(8,128)(2,1)S(1)} %pad_maximum_fusion.refs_0_), channel_id=1, source_target_pairs={{0,64},{64,0},{1,65},{65,1},{2,66},{66,2},{3,67},{67,3},{4,68},{68... | collective-permute-start | bytes 1572872 | tf_op jit(solution)/shard_map/ppermute | solution.py:189
  104.4 17.1 %collective-permute-start.17 = (bf16[4,2,64,512]{3,2,1,0:T(8,128)(2,1)S(1)}, bf16[4,2,64,512]{3,2,1,0:T(8,128)(2,1)}, u32[]{:S(2)}, u32[]{:S(2)}) collective-permute-start(bf16[4,2,64,512]{3,2,1,0:T(8,128)(2,1)S(1)} %collective-permute-done.13.refs_3_), channel_id=1, source_target_pairs={{0,64},{64,0},{1,65},{65,1},{2,66},{66,2},{3,67},{67,3},{4,68},{68... | collective-permute-start | bytes 1572872 | tf_op jit(solution)/shard_map/ppermute | solution.py:189
  109.7 11.8 %collective-permute-start.16 = (bf16[4,2,64,512]{3,2,1,0:T(8,128)(2,1)S(1)}, bf16[4,2,64,512]{3,2,1,0:T(8,128)(2,1)}, u32[]{:S(2)}, u32[]{:S(2)}) collective-permute-start(bf16[4,2,64,512]{3,2,1,0:T(8,128)(2,1)S(1)} %collective-permute-done.12.refs_2_), channel_id=1, source_target_pairs={{0,64},{64,0},{1,65},{65,1},{2,66},{66,2},{3,67},{67,3},{4,68},{68... | collective-permute-start | bytes 1572872 | tf_op jit(solution)/shard_map/ppermute | solution.py:189
  113.7 7.8 %collective-permute-start.15 = (bf16[4,2,64,512]{3,2,1,0:T(8,128)(2,1)S(1)}, bf16[4,2,64,512]{3,2,1,0:T(8,128)(2,1)}, u32[]{:S(2)}, u32[]{:S(2)}) collective-permute-start(bf16[4,2,64,512]{3,2,1,0:T(8,128)(2,1)S(1)} %collective-permute-done.11.refs_1_), channel_id=1, source_target_pairs={{0,64},{64,0},{1,65},{65,1},{2,66},{66,2},{3,67},{67,3},{4,68},{68... | collective-permute-start | bytes 1572872 | tf_op jit(solution)/shard_map/ppermute | solution.py:189
